TPU v7x, 512 devices: a whole 4x8x8 slice. The times are simulated.
512 devices in a mesh: blk: 32 (over x_hi, y, core), grp: 16 (over z, x_lo).
Axes of the slice: x: 4 (x_hi: 2, x_lo: 2; x = x_hi * 2 + x_lo), y: 8, z: 8, core: 2. Of those that a mesh axis runs over, the one named last changes fastest.
Arguments:
- users: float32 [65536, 256], P(('blk', 'grp'))
- items: float32 [16384, 256], P(('blk', 'grp'))
- counts: int32 [16384], P(('blk', 'grp')), may hold values from 50 to 15000
- target_indices: int32 [65536], P(('blk', 'grp')), may hold values from 0 to 16383, as said below
Outputs:
- loss: float32 [], replicated
- query_tower_slope: float32 [65536, 256], P(('blk', 'grp'))
- candidate_tower_slope: float32 [16384, 256], P(('blk', 'grp'))
Inputs may be any that keep to these rules, and one draw needn't show every extreme that they name: `target_indices`: user rows of the k-th aligned block of 128 rows name items of the k-th aligned block of 32 items, each such item named by exactly 4 of them.
All inputs are finite; a program needn't handle non-finite values.
Results may differ from a plain program's by a relative error of at most 0.012.
The roundings to bfloat16 on the way count: a program that leaves them out, or rounds other values in their place, can miss the bound.
Values may be sent and summed in bfloat16 or wider, within the bound.
A program may use at most 64 MiB of HBM per device.

v0:
```python
import jax
import jax.numpy as jnp
from jax import lax
from jax.sharding import PartitionSpec as P

scaling_divisor = 5.0


def joined(x, axis, combine):
    everything = jax.tree.map(lambda part: lax.all_gather(part, axis), x)
    leading = jax.tree.map(lambda part: part[0], everything)

    def step(k, so_far):
        return combine(so_far, jax.tree.map(lambda part: part[k], everything))

    return lax.fori_loop(1, lax.axis_size(axis), step, leading)


def piece_length(total):
    length = min(total, 512)
    while total % length != 0:
        length = length - 1
    return length


def combine_stats(first_vectors, second):
    top = jnp.maximum(first_vectors[0], second[0])
    return (
        top,
        first_vectors[1] * jnp.exp(first_vectors[0] - top) + second[1] * jnp.exp(second[0] - top),
    )


def split_pieces(item_block, logq_block):
    length = piece_length(item_block.shape[0])
    pieces = item_block.reshape(-1, length, item_block.shape[1])
    logq_pieces = logq_block.reshape(-1, length)
    return (pieces, logq_pieces)


def piece_scores(user_block, piece_rows, piecewise_chance_logarithm):
    score_table = jnp.einsum(
        "ud,id->ui", user_block, piece_rows, preferred_element_type=jnp.float32
    )
    return score_table / scaling_divisor - piecewise_chance_logarithm.astype(jnp.float32)[None, :]


def empty_stats(count_users):
    return (jnp.full((count_users,), -jnp.inf, jnp.float32), jnp.zeros((count_users,), jnp.float32))


def local_stats(user_block, item_block, logq_block):
    pieces, logq_pieces = split_pieces(item_block, logq_block)

    def visit(carry, entry):
        score_table = piece_scores(user_block, entry[0], entry[1])
        top = jnp.max(score_table, axis=1)
        total = jnp.sum(jnp.exp(score_table - top[:, None]), axis=1)
        return (combine_stats(carry, (top, total)), None)

    stats, unused = lax.scan(visit, empty_stats(user_block.shape[0]), (pieces, logq_pieces))
    return stats


def local_grads(user_block, item_block, logq_block, lse):
    pieces, logq_pieces = split_pieces(item_block, logq_block)

    def visit(user_total, entry):
        score_table = piece_scores(user_block, entry[0], entry[1])
        weights = jnp.exp(score_table - lse[:, None]).astype(jnp.bfloat16)
        user_total = user_total + jnp.dot(weights, entry[0], preferred_element_type=jnp.float32)
        item_piece = jnp.einsum(
            "ui,ud->id", weights, user_block, preferred_element_type=jnp.float32
        )
        return (user_total, item_piece)

    start = jnp.zeros(user_block.shape, jnp.float32)
    user_total, item_parts = lax.scan(visit, start, (pieces, logq_pieces))
    return (user_total, item_parts.reshape(item_block.shape))


def on_device(users, items, counts, target_indices):
    count_users = users.shape[0]
    count_items = items.shape[0]
    user_half = users.astype(jnp.bfloat16)
    candidate_midpoint = items.astype(jnp.bfloat16)
    draw_chance_logarithm = jnp.log(counts.astype(jnp.float32)).astype(jnp.bfloat16)
    user_block = lax.all_gather(user_half, "grp", axis=0, tiled=True)
    item_block, logq_block = (
        lax.all_gather(candidate_midpoint, "blk", axis=0, tiled=True),
        lax.all_gather(draw_chance_logarithm, "blk", axis=0, tiled=True),
    )
    stats = local_stats(user_block, item_block, logq_block)
    top, total = joined(stats, "grp", combine_stats)
    lse = top + jnp.log(total)
    user_part, item_part = local_grads(user_block, item_block, logq_block, lse)
    candidate_accumulator = lax.psum_scatter(item_part, "blk", scatter_dimension=0, tiled=True)
    query_accumulator = lax.psum_scatter(user_part, "grp", scatter_dimension=0, tiled=True)
    own_lse = lax.dynamic_slice_in_dim(lse, lax.axis_index("grp") * count_users, count_users)
    first_item = (
        lax.axis_index("blk") * lax.axis_size("grp") + lax.axis_index("grp")
    ) * count_items
    local_pos = target_indices - first_item
    match = (local_pos[:, None] == jnp.arange(count_items, dtype=jnp.int32)[None, :]).astype(
        jnp.float32
    )
    query_whole = user_half.astype(jnp.float32)
    item_full = candidate_midpoint.astype(jnp.float32)
    target_candidate_vectors = jnp.dot(match, item_full, precision=lax.Precision.HIGHEST)
    positive_log_prob = jnp.dot(
        match, draw_chance_logarithm.astype(jnp.float32), precision=lax.Precision.HIGHEST
    )
    target_query_vectors = jnp.dot(match.T, query_whole, precision=lax.Precision.HIGHEST)
    target_score = (
        jnp.sum(query_whole * target_candidate_vectors, axis=1) / scaling_divisor
        - positive_log_prob
    )
    loss_total = lax.psum(jnp.sum(own_lse - target_score), ("blk", "grp"))
    loss = loss_total / (count_users * lax.axis_size("blk") * lax.axis_size("grp"))
    query_tower_slope = (query_accumulator - target_candidate_vectors) / scaling_divisor
    candidate_tower_slope = (candidate_accumulator - target_query_vectors) / scaling_divisor
    return (loss, query_tower_slope, candidate_tower_slope)


def solution(mesh):
    placed = (
        P(("blk", "grp"), None),
        P(("blk", "grp"), None),
        P(("blk", "grp")),
        P(("blk", "grp")),
    )
    return jax.shard_map(
        on_device,
        mesh=mesh,
        in_specs=placed,
        out_specs=(P(), P(("blk", "grp"), None), P(("blk", "grp"), None)),
        check_vma=False,
    )
```

profile of v0, /device:TPU:24, one launch (start us, length us, event | category | flops | bytes accessed | tf_op | source)
XLA Modules:
  0.0 418.2 jit_solution(501176503268834922)
XLA Ops:
  7.2 0.0 all-gather.4.cloned.1.call-start
  7.2 0.8 convert_element_type.23
  8.0 0.7 broadcast_subtract_fusion
  8.6 1.6 multiply_reduce_fusion
  10.3 0.0 all-gather.4.cloned.1.call-update
  10.3 0.0 reduce-scatter.5.cloned.1.call-start
  10.4 1.3 dynamic-slice
  12.4 0.7 log_convert_fusion
  13.0 0.2 dynamic-update-slice
  13.2 54.2 %all-reduce = bf16[1024]{0:T(1024)(128)(2,1)S(1)} all-reduce(bf16[1024]{0:T(1024)(128)(2,1)S(1)} %dynamic-update-slice), channel_id=1, replica_groups=mesh['blk'=32,'grp'=16] {'blk'}, use_global_device_ids=true, to_apply=%add | all-reduce | flops 1024 | bytes 4096
  67.5 52.6 %all_gather.21 = bf16[1024,256]{1,0:T(8,128)(2,1)} all-gather(bf16[32,256]{1,0:T(8,128)(2,1)S(1)} %convert_element_type.23), channel_id=1, replica_groups=mesh['blk'=32,'grp'=16] {'blk'}, dimensions={0}, use_global_device_ids=true | all-gather | bytes 540672 | tf_op jit(solution)/shard_map/all_gather | solution.py:90
  120.1 0.0 all-gather.4.cloned.1.call-done
  120.1 6.1 %while.44 = (s32[]{:T(128)}, f32[2048]{0:T(1024)S(1)}, f32[2048]{0:T(1024)S(1)}, bf16[2,512,256]{2,1,0:T(8,128)(2,1)}, bf16[2048,256]{1,0:T(8,128)(2,1)}, /*index=5*/bf16[2,512]{1,0:T(2,128)(2,1)S(1)}, s32[]{:T(128)}, s32[]{:T(128)}) while((s32[]{:T(128)}, f32[2048]{0:T(1024)S(1)}, f32[2048]{0:T(1024)S(1)}, ...), condition=%wide.region_3.4_spmd.clone, body=%wide.region_0.3_spmd.clone.sunk | while | flops 544223744 | bytes 9780335 | solution.py:61
  120.1 2.1 fusion.40
  122.1 0.9 exponential_reduce_fusion.2
  123.1 2.1 fusion.40
  125.2 0.9 exponential_reduce_fusion.2
  126.1 39.3 %all-gather.1 = f32[32768]{0:T(1024)S(1)} all-gather(f32[2048]{0:T(1024)S(1)} %get-tuple-element.208), channel_id=3, replica_groups=mesh['blk'=32,'grp'=16] {'grp'}, dimensions={0}, use_global_device_ids=true | all-gather | bytes 139264 | tf_op jit(solution)/shard_map/all_gather | solution.py:10
  165.5 30.3 %all-gather = f32[32768]{0:T(1024)S(1)} all-gather(f32[2048]{0:T(1024)S(1)} %get-tuple-element.207), channel_id=2, replica_groups=mesh['blk'=32,'grp'=16] {'grp'}, dimensions={0}, use_global_device_ids=true | all-gather | bytes 139264 | tf_op jit(solution)/shard_map/all_gather | solution.py:10
  195.8 1.0 while.43
  196.8 0.0 copy-start.5
  196.8 0.0 copy-start.4
  196.8 12.1 %while.45 = (s32[]{:T(128)}, f32[2048,256]{1,0:T(8,128)S(1)}, f32[2,512,256]{2,1,0:T(8,128)}, bf16[2,512,256]{2,1,0:T(8,128)(2,1)}, bf16[2048,256]{1,0:T(8,128)(...) while((s32[]{:T(128)}, f32[2048,256]{1,0:T(8,128)S(1)}, ...), condition=%wide.region_10.11_spmd.clone, body=%wide.region_9.10_spmd.clone.sunk | while | flops 1615856128 | bytes 26227924 | solution.py:78
  196.8 0.0 copy-start.1
  196.9 0.0 copy-start.2
  196.9 2.5 exponential_convert_fusion.2
  199.4 0.0 copy-done.1
  199.4 0.0 copy-done.2
  199.4 0.7 fusion.48
  200.1 0.0 copy-start.3
  200.1 2.7 convolution_add_fusion.2
  202.9 0.0 copy-done.3
  202.9 0.0 copy-start.1
  202.9 0.0 copy-start.2
  202.9 2.5 exponential_convert_fusion.2
  205.4 0.0 copy-done.1
  205.4 0.0 copy-done.2
  205.4 0.7 fusion.48
  206.1 0.0 copy-start.3
  206.2 2.7 convolution_add_fusion.2
  208.9 0.0 copy-done.3
  208.9 0.0 copy-start
  208.9 0.0 reduce-scatter.5.cloned.1.call-update
  208.9 0.0 reduce-scatter.3.cloned.1.call-start
  209.0 1.3 copy-done
  210.2 0.0 reduce-scatter.3.cloned.1.call-update
  210.3 0.0 copy-done.5
  210.3 0.8 fusion.16
  211.1 97.1 %psum.7 = f32[]{:T(128)} all-reduce(f32[]{:T(128)} %fusion.16), channel_id=1, replica_groups=mesh['blk'=32,'grp'=16] {'blk','grp'}, use_global_device_ids=true, to_apply=%region_8.9 | all-reduce | flops 1 | bytes 8 | tf_op jit(solution)/shard_map/psum | solution.py:118
  308.8 18.6 %reduce-scatter.5.cloned.1.call-done = f32[32,256]{1,0:T(8,128)} async-done(((f32[1024,256]{1,0:T(8,128)}), f32[32,256]{1,0:T(8,128)}) %reduce-scatter.5.cloned.1.call-update) | async-done | bytes 32784 | tf_op jit(solution)/shard_map/reduce_scatter | solution.py:97
  327.4 0.0 copy-done.4
  327.4 1.6 fusion.13
  329.1 79.9 %reduce-scatter.3.cloned.1.call-done = f32[128,256]{1,0:T(8,128)} async-done(((f32[2048,256]{1,0:T(8,128)}), f32[128,256]{1,0:T(8,128)}) %reduce-scatter.3.cloned.1.call-update) | async-done | bytes 131088 | tf_op jit(solution)/shard_map/reduce_scatter | solution.py:98
  408.9 1.6 subtract_multiply_fusion
  (47 shorter events, 0.7 us)
Async XLA Ops:
  7.2 112.9 %all-gather.4.cloned.1.call-start = ((), (), s32[]{:S(2)}) async-start(), calls=%async_computation.2 | async-start | bytes 1114112 | tf_op jit(solution)/shard_map/all_gather | solution.py:88
  10.3 317.1 %reduce-scatter.5.cloned.1.call-start = ((), (), s32[]{:S(2)}) async-start(), calls=%async_computation.4 | async-start | bytes 1081344 | tf_op jit(solution)/shard_map/reduce_scatter | solution.py:97
  196.8 13.5 %copy-start.5 = (s32[32]{0:T(128)S(1)}, s32[32]{0:T(128)}, u32[]{:S(2)}) copy-start(s32[32]{0:T(128)} %param.12) | copy-start | bytes 388
  196.8 130.6 %copy-start.4 = (bf16[128,256]{1,0:T(8,128)(2,1)S(1)}, bf16[128,256]{1,0:T(8,128)(2,1)}, u32[]{:S(2)}) copy-start(bf16[128,256]{1,0:T(8,128)(2,1)} %get-tuple-element.299) | copy-start | bytes 196612
  196.8 2.5 copy-start.1
  196.9 2.5 copy-start.2
  200.1 2.7 copy-start.3
  202.9 2.5 copy-start.1
  202.9 2.5 copy-start.2
  206.1 2.7 copy-start.3
  208.9 1.4 copy-start
  208.9 200.0 %reduce-scatter.3.cloned.1.call-start = ((), (), s32[]{:S(2)}) async-start(), calls=%async_computation.3 | async-start | bytes 2228224 | tf_op jit(solution)/shard_map/reduce_scatter | solution.py:98
Sparse Core Ops, SparseCore 0:
  10.7 76.2 all-gather.3
  209.0 118.3 reduce-scatter.4
  330.5 78.4 reduce-scatter.2
where the time goes:
time: 419 us; the launch traced here: 418 us
  blocking collectives  273 us (65%)
  waiting for transfers between devices  98.5 us (24%)
  matrix products  20.1 us (5%)
  between operations  16.3 us (4%)
  other arithmetic  5.73 us (1%)
    psum x1, blocking collectives, on_device(): loss_total = lax.psum(jnp.sum(own_lse - target_score), ('blk', 'grp'))  97.1 us
    reduce_scatter x1, waiting for transfers between devices, on_device(): lax.psum_scatter(user_part, 'grp', scatter_dimension=0, tiled=True)  79.9 us
    all_gather x2, blocking collectives, joined(): everything = jax.tree.map(lambda part: lax.all_gather(part, axis), x)  69.6 us
    unnamed x1, blocking collectives  54.2 us
    all_gather x1, blocking collectives, on_device(): lax.all_gather(candidate_midpoint, 'blk', axis=0, tiled=True)  52.6 us
    reduce_scatter x1, waiting for transfers between devices, on_device(): lax.psum_scatter(item_part, 'blk', scatter_dimension=0, tiled=True)  18.6 us
    dot_general x4, matrix products, piece_scores(): jnp.einsum('ud,id->ui', user_block, piece_rows, preferred_element_type=jn...  9.1 us
  transfers between devices with their start and end apart: 3, of which 2 were waited for; matrix products, arithmetic and copies ran while one was open for 1% of the time, Pallas kernels for 0%

commit v1 on v0

v1 whole, which is shorter than its diff:
```python
import functools
import math

import jax
import jax.numpy as jnp
from jax import lax
from jax.experimental import pallas as pl
from jax.experimental.pallas import tpu as pltpu
from jax.sharding import PartitionSpec as P

scaling_divisor = 5.0
LOG2E = math.log2(math.e)
LN2 = math.log(2.0)
MESH = pl.DeviceIdType.MESH
BF16 = jnp.bfloat16
F32 = jnp.float32

NX, NY, NZ = 4, 8, 8
UD, ID, D = 128, 32, 256
ORDER = (0, 1, 7, 2, 6, 3, 5, 4)
SLOT = tuple(ORDER.index(k) for k in range(NY))
HALF = NX * NY * ID // 2


def offset_of(k):
    return jnp.where(k % 2 == 1, (k + 1) // 2, (8 - k // 2) % 8)


def dot(a, b, ca=1, cb=0):
    return lax.dot_general(a, b, (((ca,), (cb,)), ((), ())), preferred_element_type=F32)


def kernel(
    users_ref, items_ref, counts_ref, tgt_ref,
    loss_ref, query_ref, cand_ref,
    rows, it, lq, it_t, lqc, p_all, acc, mst, lst, st_out, st_in, pt_out, pt_in,
    w_row, own_f, ip, xc_in, xs_in, ys_out, ys_in, loss_out, loss_in, tq_s, tv_s,
    z_ss, z_rs, y_ss, y_rs, ql_ss, ql_rs, x_ss, x_rs, qx_ss, qx_rs, c_ss, c_rs,
    st_ss, st_rs, pt_ss, pt_rs, xc_ss, xc_rs, xs_ss, xs_rs, ys_ss, ys_rs, ls_ss, ls_rs,
):
    b = lax.axis_index("blk")
    g = lax.axis_index("grp")
    x = (b // 16) * 2 + g % 2
    y = (b // 2) % 8
    z = g // 2
    core = b % 2

    def device(dx=0, dy=0, dz=0, dc=0):
        xx = (x + dx) % NX
        return (
            ((xx // 2) * 8 + (y + dy) % NY) * 2 + (core + dc) % 2,
            ((z + dz) % NZ) * 2 + xx % 2,
        )

    def copy(src, dst, ss, rs, **to):
        return pltpu.make_async_remote_copy(
            src_ref=src, dst_ref=dst, send_sem=ss, recv_sem=rs,
            device_id=device(**to), device_id_type=MESH,
        )

    barrier = pltpu.get_barrier_semaphore()
    for d in range(1, NZ):
        pl.semaphore_signal(barrier, inc=1, device_id=device(dz=d), device_id_type=MESH)
    for d in range(1, NY):
        pl.semaphore_signal(barrier, inc=1, device_id=device(dy=d), device_id_type=MESH)
    for d in range(1, NX):
        pl.semaphore_signal(barrier, inc=1, device_id=device(dx=d), device_id_type=MESH)
    pl.semaphore_signal(barrier, inc=1, device_id=device(dc=1), device_id_type=MESH)

    rows[0] = users_ref[...].astype(BF16)
    it[0, 0:ID, :] = items_ref[...].astype(BF16)
    logq = jnp.log(counts_ref[...].astype(F32)).astype(BF16).astype(F32)
    logq = jnp.concatenate([logq, jnp.zeros((1, 128 - ID), F32)], axis=1)
    lq[0, 0, 0] = logq

    pl.semaphore_wait(barrier, NZ + NY + NX - 3 + 1)

    def z_copy(d):
        return copy(rows.at[0], rows.at[(NZ - d) % NZ], z_ss.at[d], z_rs.at[(NZ - d) % NZ], dz=d)

    def y_copy(d):
        s = SLOT[(NY - d) % NY]
        return copy(
            it.at[0, pl.ds(0, ID)], it.at[0, pl.ds(s * NX * ID, ID)], y_ss.at[d], y_rs.at[s], dy=d
        )

    def ql_copy(d):
        s = SLOT[(NY - d) % NY]
        return copy(lq.at[0, 0, 0], lq.at[0, s, 0], ql_ss.at[d], ql_rs.at[s], dy=d)

    def x_copy(s, e):
        return copy(
            it.at[0, pl.ds(s * NX * ID, ID)],
            it.at[0, pl.ds((s * NX + NX - e) * ID, ID)],
            x_ss.at[s, e], x_rs.at[s, NX - e], dx=e,
        )

    def qx_copy(e):
        return copy(lq.at[0, :, 0], lq.at[0, :, NX - e], qx_ss.at[e], qx_rs.at[NX - e], dx=e)

    def c_copy(h):
        part = pl.ds(h * HALF, HALF)
        return copy(it.at[0, part], it.at[1, part], c_ss.at[h], c_rs.at[h], dc=1)

    def qc_copy():
        return copy(lq.at[0], lq.at[1], c_ss.at[2], c_rs.at[2], dc=1)

    for d in ORDER[1:]:
        ql_copy(d).start()
        y_copy(d).start()
        z_copy(d).start()
    for e in range(1, NX):
        x_copy(0, e).start()

    first = (b * 16 + g) * ID
    hot = (
        lax.broadcasted_iota(jnp.int32, (ID, UD), 0) + first == tgt_ref[...]
    ).astype(F32)
    hot_half = hot.astype(BF16)
    own_items = it[0, 0:ID, :]
    tq = dot(hot_half, rows[0])
    tq_s[...] = tq
    tv_s[...] = dot(own_items, hot_half, 0, 0)
    eye = (
        lax.broadcasted_iota(jnp.int32, (ID, 128), 0)
        == lax.broadcasted_iota(jnp.int32, (ID, 128), 1)
    )
    own_logq = jnp.where(eye, jnp.broadcast_to(logq, (ID, 128)), 0.0)
    named = jnp.sum(hot, axis=1, keepdims=True)
    pos = jnp.sum(
        jnp.sum(tq * own_items.astype(F32), axis=1, keepdims=True) * (1.0 / scaling_divisor)
        - jnp.sum(own_logq, axis=1, keepdims=True) * named,
        axis=0, keepdims=True,
    )
    st_out[1] = jnp.broadcast_to(pos, (8, 128))

    def forward(s, carry):
        pltpu.make_async_copy(
            it.at[0, pl.ds(0, ID)], it.at[0, pl.ds(s * NX * ID, ID)], y_rs.at[s]
        ).wait()
        for e in range(1, NX):
            x_copy(s, e).start()
        return carry

    lax.fori_loop(1, 4, forward, 0)
    for s in range(1, NY):
        pltpu.make_async_copy(lq.at[0, 0, 0], lq.at[0, s, 0], ql_rs.at[s]).wait()
    for e in range(1, NX):
        qx_copy(e).start()
    lax.fori_loop(4, 8, forward, 0)
    for e in range(1, NX):
        pltpu.make_async_copy(lq.at[0, :, 0], lq.at[0, :, e], qx_rs.at[e]).wait()
    qc_copy().start()

    def arrived(s, carry):
        for e in range(1, NX):
            spot = it.at[0, pl.ds((s * NX + e) * ID, ID)]
            pltpu.make_async_copy(spot, spot, x_rs.at[s, e]).wait()
        return carry

    ones = jnp.ones((128, 128), BF16)

    def prepare(blk):
        side, half = blk // 2, blk % 2
        it_t[blk] = it[side, half * HALF : (half + 1) * HALF, :].T

        def column(i, carry):
            row = jnp.broadcast_to(lq[side, half * 4 + i // 4, i % 4], (ID, 128))
            spread = jnp.where(eye, row, 0.0).astype(BF16)
            lqc[blk, pl.ds(pl.multiple_of(i * ID, ID), ID), :] = dot(spread, ones) * LOG2E
            return carry

        lax.fori_loop(0, 16, column, 0)

    def unit(blk, s):
        side, half = blk // 2, blk % 2
        scores = dot(
            it[side, pl.ds(pl.multiple_of(half * HALF, HALF), HALF), :], rows[s], 1, 1
        )
        t = scores * (LOG2E / scaling_divisor) - lqc[blk]
        m = jnp.max(t, axis=0, keepdims=True)
        p = jnp.exp2(t - m)
        mst[blk, pl.ds(s, 1), :] = m
        lst[blk, pl.ds(s, 1), :] = jnp.sum(p, axis=0, keepdims=True)
        p = p.astype(BF16)
        p_all[blk, :, pl.ds(pl.multiple_of(s * UD, UD), UD)] = p
        acc[blk, s] = dot(it_t[blk], p)

    def wait_users(k):
        s = offset_of(k)
        pltpu.make_async_copy(rows.at[0], rows.at[s], z_rs.at[s]).wait()

    def early(blk):
        def step(k, carry):
            unit(blk, offset_of(k))
            return carry

        lax.fori_loop(0, 3, step, 0)

    lax.fori_loop(0, 4, arrived, 0)
    c_copy(0).start()
    prepare(0)
    wait_users(1)
    wait_users(2)
    early(0)
    lax.fori_loop(4, 8, arrived, 0)
    c_copy(1).start()
    prepare(1)
    early(1)
    qc_copy().wait_recv()
    c_copy(0).wait_recv()
    prepare(2)
    early(2)
    c_copy(1).wait_recv()
    prepare(3)
    early(3)

    def late(k, carry):
        wait_users(k)

        def step(blk, carry):
            unit(blk, offset_of(k))
            return carry

        return lax.fori_loop(0, 4, step, carry)

    lax.fori_loop(3, 8, late, 0)

    top = jnp.max(mst[...], axis=0)
    local = top + jnp.log2(sum(lst[k] * jnp.exp2(mst[k] - top) for k in range(4)))
    st_out[0] = local

    def st_copy(d):
        return copy(st_out, st_in.at[(NZ - d) % NZ], st_ss.at[d], st_rs.at[(NZ - d) % NZ], dz=d)

    def pt_copy(d):
        return copy(
            pt_out.at[d], pt_in.at[(NZ - d) % NZ], pt_ss.at[d], pt_rs.at[(NZ - d) % NZ], dz=d
        )

    for d in (4, 3, 5, 2, 6, 1, 7):
        st_copy(d).start()

    for k in range(4):
        lst[k] = jnp.exp2(mst[k] - local)

    def part_of(s):
        return sum(acc[k, s] * lst[k, pl.ds(s, 1), :] for k in range(4))

    def give(s, carry):
        pt_out[s] = part_of(s).astype(BF16)
        pt_copy(s).start()
        return carry

    lax.fori_loop(1, NZ, give, 0)

    for e in range(1, NZ):
        pltpu.make_async_copy(st_out, st_in.at[e], st_rs.at[e]).wait()
    seen = [local] + [jnp.roll(st_in[e, 0], e, axis=0) for e in range(1, NZ)]
    top = functools.reduce(jnp.maximum, seen)
    lse = top + jnp.log2(sum(jnp.exp2(v - top) for v in seen))
    share = [jnp.exp2(v[0:1] - lse[0:1]) for v in seen]
    for k in range(4):
        w = jnp.exp2(mst[k] - lse).astype(BF16)
        for s in range(NZ):
            w_row[k, :, s * UD : (s + 1) * UD] = w[s : s + 1, :]

    def item_part(blk, c):
        chunk = pl.ds(pl.multiple_of(c * 128, 128), 128)
        weights = p_all[blk, chunk, :] * w_row[blk]
        return dot(weights, rows[...].reshape(NZ * UD, D))

    def xc_copy(h):
        part = pl.ds(h * HALF, HALF)
        return copy(ip.at[1, part], xc_in.at[part], xc_ss.at[h], xc_rs.at[h], dc=1)

    for h in (1, 0):
        def other(c, carry):
            spot = pl.ds(pl.multiple_of(h * HALF + c * 128, 128), 128)
            ip[1, spot, :] = item_part(2 + h, c).astype(BF16)
            return carry

        lax.fori_loop(0, 4, other, 0)
        xc_copy(h).start()

    for h in (1, 0):
        def own(c, carry):
            spot = pl.ds(pl.multiple_of(h * HALF + c * 128, 128), 128)
            own_f[spot, :] = item_part(h, c)
            return carry

        lax.fori_loop(0, 4, own, 0)

    def ls_copy(i, j, **to):
        return copy(loss_out.at[i], loss_in.at[j], ls_ss.at[j], ls_rs.at[j], **to)

    pos_all = st_out[1] + sum(st_in[e, 1] for e in range(1, NZ))
    line = jnp.sum(jnp.sum(lse, axis=1, keepdims=True), axis=0, keepdims=True) * LN2
    loss_out[0] = jnp.broadcast_to(line, (8, 128)) - pos_all
    ls_copy(0, 0, dc=1).start()

    def xs_copy(s, e):
        return copy(
            ip.at[0, pl.ds((s * NX + e) * ID, ID)], xs_in.at[s, NX - e],
            xs_ss.at[s, e], xs_rs.at[s, NX - e], dx=e,
        )

    for h in (1, 0):
        xc_copy(h).wait_recv()

        def own_sum(s, carry):
            spot = pl.ds(pl.multiple_of(s * NX * ID, NX * ID), NX * ID)
            total = own_f[spot, :] + xc_in[spot, :].astype(F32)
            own_f[spot, :] = total
            ip[0, spot, :] = total.astype(BF16)
            for e in (2, 1, 3):
                xs_copy(s, e).start()
            return carry

        lax.fori_loop(h * 4, h * 4 + 4, own_sum, 0)

    ls_copy(0, 0, dc=1).wait_recv()
    loss_out[1] = loss_out[0] + loss_in[0]
    for e in range(1, NX):
        ls_copy(1, e, dx=e).start()

    def ys_copy(s):
        o = offset_of(s)
        mirror = jnp.where(s == 0, 0, jnp.where(s == 7, 7, jnp.where(s % 2 == 1, s + 1, s - 1)))
        return copy(ys_out.at[s], ys_in.at[mirror], ys_ss.at[s], ys_rs.at[mirror], dy=o)

    def x_total(s):
        for e in range(1, NX):
            pltpu.make_async_copy(xs_in.at[s, e], xs_in.at[s, e], xs_rs.at[s, e]).wait()
        spot = pl.ds(pl.multiple_of(s * NX * ID, NX * ID), ID)
        return own_f[spot, :] + sum(xs_in[s, e].astype(F32) for e in range(1, NX))

    def relay(i, carry):
        s = 7 - i
        ys_out[s] = x_total(s).astype(BF16)
        ys_copy(s).start()
        return carry

    lax.fori_loop(0, 7, relay, 0)
    for e in range(1, NX):
        ls_copy(1, e, dx=e).wait_recv()
    loss_out[2] = loss_out[1] + loss_in[1] + loss_in[2] + loss_in[3]
    for d in range(1, NY):
        ls_copy(2, 3 + d, dy=d).start()
    cand = x_total(0) - tq_s[...]

    user_sum = part_of(0) * share[0] - tv_s[...]
    for e in range(1, NZ):
        pltpu.make_async_copy(pt_in.at[e], pt_in.at[e], pt_rs.at[e]).wait()
        user_sum = user_sum + pt_in[e].astype(F32) * share[e]
    query_ref[...] = user_sum.T * (1.0 / scaling_divisor)

    for s in range(1, NY):
        pltpu.make_async_copy(ys_in.at[s], ys_in.at[s], ys_rs.at[s]).wait()
        cand = cand + ys_in[s].astype(F32)
    cand_ref[...] = cand * (1.0 / scaling_divisor)
    total = loss_out[2]
    for d in range(1, NY):
        ls_copy(2, 3 + d, dy=d).wait_recv()
        total = total + loss_in[3 + d]
    users_all = 2 * NX * NY * NZ * UD
    loss_ref[...] = total[0:1, 0:1] * (1.0 / users_all)

    for d in range(1, NZ):
        z_copy(d).wait_send()
        y_copy(d).wait_send()
        ql_copy(d).wait_send()
        st_copy(d).wait_send()
        pt_copy(d).wait_send()
        ls_copy(2, 3 + d, dy=d).wait_send()
    for e in range(1, NX):
        qx_copy(e).wait_send()
        ls_copy(1, e, dx=e).wait_send()

    def left(s, carry):
        for e in range(1, NX):
            x_copy(s, e).wait_send()
            xs_copy(s, e).wait_send()
        return carry

    lax.fori_loop(0, NY, left, 0)

    def left_y(s, carry):
        ys_copy(s).wait_send()
        return carry

    lax.fori_loop(1, NY, left_y, 0)
    for h in range(2):
        c_copy(h).wait_send()
        xc_copy(h).wait_send()
    qc_copy().wait_send()
    ls_copy(0, 0, dc=1).wait_send()


def on_device(users, items, counts, target_indices):
    dma = lambda *n: pltpu.SemaphoreType.DMA(n)
    pair = lambda *n: [dma(*n), dma(*n)]
    vmem = pl.BlockSpec(memory_space=pltpu.VMEM)
    loss, query, cand = pl.pallas_call(
        kernel,
        out_shape=(
            jax.ShapeDtypeStruct((1, 1), F32),
            jax.ShapeDtypeStruct((UD, D), F32),
            jax.ShapeDtypeStruct((ID, D), F32),
        ),
        in_specs=[vmem] * 4,
        out_specs=(vmem,) * 3,
        scratch_shapes=[
            pltpu.VMEM((NZ, UD, D), BF16),
            pltpu.VMEM((2, 2 * HALF, D), BF16),
            pltpu.VMEM((2, NY, NX, 1, 128), F32),
            pltpu.VMEM((4, D, HALF), BF16),
            pltpu.VMEM((4, HALF, 128), F32),
            pltpu.VMEM((4, HALF, NZ * UD), BF16),
            pltpu.VMEM((4, NZ, D, UD), F32),
            pltpu.VMEM((4, NZ, UD), F32),
            pltpu.VMEM((4, NZ, UD), F32),
            pltpu.VMEM((2, 8, 128), F32),
            pltpu.VMEM((NZ, 2, 8, 128), F32),
            pltpu.VMEM((NZ, D, UD), BF16),
            pltpu.VMEM((NZ, D, UD), BF16),
            pltpu.VMEM((4, 1, NZ * UD), BF16),
            pltpu.VMEM((2 * HALF, D), F32),
            pltpu.VMEM((2, 2 * HALF, D), BF16),
            pltpu.VMEM((2 * HALF, D), BF16),
            pltpu.VMEM((NY, NX, ID, D), BF16),
            pltpu.VMEM((NY, ID, D), BF16),
            pltpu.VMEM((NY, ID, D), BF16),
            pltpu.VMEM((3, 8, 128), F32),
            pltpu.VMEM((11, 8, 128), F32),
            pltpu.VMEM((ID, D), F32),
            pltpu.VMEM((D, UD), F32),
            *pair(NZ), *pair(NY), *pair(NY), *pair(NY, NX), *pair(NX), *pair(3),
            *pair(NZ), *pair(NZ), *pair(2), *pair(NY, NX), *pair(NY), *pair(11),
        ],
        compiler_params=pltpu.CompilerParams(
            collective_id=0, has_side_effects=True, vmem_limit_bytes=48 * 2**20
        ),
        cost_estimate=pl.CostEstimate(
            flops=6 * 1024 * 2048 * D, bytes_accessed=2**19, transcendentals=1024 * 2048
        ),
        name="towers",
    )(users, items, counts.reshape(1, ID), target_indices.reshape(1, UD))
    return loss.reshape(()), query, cand


def solution(mesh):
    placed = P(("blk", "grp"))
    wide = P(("blk", "grp"), None)
    return jax.shard_map(
        on_device,
        mesh=mesh,
        in_specs=(wide, wide, placed, placed),
        out_specs=(P(), wide, wide),
        check_vma=False,
    )
```

time: 419 us -> 82 us (0.20)
  the two profiles are of different devices: /device:TPU:24 before, /device:TPU:2 now
where the time goes in v1:
time: 82 us; the launch traced here: 81.8 us
  Pallas kernels  75.8 us (92%)
  local copies, waits for them, and re-layouts  3.59 us (4%)
  between operations  2.4 us (3%)
    pallas_call x1, Pallas kernels, on_device(): pl.pallas_call(kernel, out_shape=(jax.ShapeDtypeStruct((1, 1), F32), jax....  75.8 us
    unnamed x10, local copies, waits for them, and re-layouts  3.59 us

profile of v1, /device:TPU:2, one launch (start us, length us, event | category | flops | bytes accessed | tf_op | source)
XLA Modules:
  0.0 81.8 jit_solution(16141754010202285524)
XLA Ops:
  0.6 0.0 copy-start.2
  0.6 0.0 copy-start.3
  0.7 0.6 copy-done.2
  1.3 0.0 copy-done.3
  1.3 0.0 copy-start
  1.3 0.9 %copy-done = f32[128,256]{1,0:T(8,128)S(1)} copy-done((f32[128,256]{1,0:T(8,128)S(1)}, f32[128,256]{1,0:T(8,128)}, u32[]{:S(2)}) %copy-start) | copy-done | bytes 131096
  2.2 0.0 copy-start.1
  2.2 0.8 copy-done.1
  3.0 75.8 %towers.1 = (f32[1,1]{1,0:T(1,128)}, f32[128,256]{1,0:T(8,128)S(1)}, f32[32,256]{1,0:T(8,128)S(1)}) custom-call(f32[128,256]{1,0:T(8,128)S(1)} %copy-done, f32[32,256]{1,0:T(8,128)S(1)} %copy-done.1, s32[1,32]{1,0:T(1,128)S(1)} %bitcast.3, s32[1,128]{1,0:T(1,128)S(1)} %bitcast.4), custom_call_target="tpu_custom_call" | custom-call | flops 3221225472 | bytes 524288 | tf_op jit(solution)/shard_map/towers/pallas_call | solution.py:404
  79.4 0.7 copy.11
  80.0 0.6 copy.12
Async XLA Ops:
  0.6 0.7 copy-start.2
  0.6 0.7 copy-start.3
  1.3 0.9 %copy-start = (f32[128,256]{1,0:T(8,128)S(1)}, f32[128,256]{1,0:T(8,128)}, u32[]{:S(2)}) copy-start(f32[128,256]{1,0:T(8,128)} %users_ref.1) | copy-start | bytes 393220
  2.2 0.8 copy-start.1

commit v2 on v1

--- a/solution.py
+++ b/solution.py
@@ -31,8 +31,9 @@
 
 
 def kernel(
-    users_ref, items_ref, counts_ref, tgt_ref,
+    users_hbm, items_hbm, counts_hbm, tgt_hbm,
     loss_ref, query_ref, cand_ref,
+    users_ref, items_ref, counts_ref, tgt_ref, in_sem,
     rows, it, lq, it_t, lqc, p_all, acc, mst, lst, st_out, st_in, pt_out, pt_in,
     w_row, own_f, ip, xc_in, xs_in, ys_out, ys_in, loss_out, loss_in, tq_s, tv_s,
     z_ss, z_rs, y_ss, y_rs, ql_ss, ql_rs, x_ss, x_rs, qx_ss, qx_rs, c_ss, c_rs,
@@ -67,6 +68,16 @@
         pl.semaphore_signal(barrier, inc=1, device_id=device(dx=d), device_id_type=MESH)
     pl.semaphore_signal(barrier, inc=1, device_id=device(dc=1), device_id_type=MESH)
 
+    loads = [
+        pltpu.make_async_copy(src, dst, in_sem.at[k])
+        for k, (src, dst) in enumerate((
+            (counts_hbm, counts_ref), (items_hbm, items_ref), (users_hbm, users_ref), (tgt_hbm, tgt_ref)
+        ))
+    ]
+    for load in loads:
+        load.start()
+    for load in loads:
+        load.wait()
     rows[0] = users_ref[...].astype(BF16)
     it[0, 0:ID, :] = items_ref[...].astype(BF16)
     logq = jnp.log(counts_ref[...].astype(F32)).astype(BF16).astype(F32)
@@ -76,7 +87,8 @@
     pl.semaphore_wait(barrier, NZ + NY + NX - 3 + 1)
 
     def z_copy(d):
-        return copy(rows.at[0], rows.at[(NZ - d) % NZ], z_ss.at[d], z_rs.at[(NZ - d) % NZ], dz=d)
+        s = SLOT[(NZ - d) % NZ]
+        return copy(rows.at[0], rows.at[s], z_ss.at[d], z_rs.at[s], dz=d)
 
     def y_copy(d):
         s = SLOT[(NY - d) % NY]
@@ -163,68 +175,56 @@
     def prepare(blk):
         side, half = blk // 2, blk % 2
         it_t[blk] = it[side, half * HALF : (half + 1) * HALF, :].T
-
-        def column(i, carry):
-            row = jnp.broadcast_to(lq[side, half * 4 + i // 4, i % 4], (ID, 128))
-            spread = jnp.where(eye, row, 0.0).astype(BF16)
-            lqc[blk, pl.ds(pl.multiple_of(i * ID, ID), ID), :] = dot(spread, ones) * LOG2E
-            return carry
-
-        lax.fori_loop(0, 16, column, 0)
-
-    def unit(blk, s):
+        row = lq[side, half * 4 : (half + 1) * 4].reshape(16, 1, 128)
+        spread = jnp.where(eye[None], jnp.broadcast_to(row, (16, ID, 128)), 0.0)
+        lqc[blk] = dot(spread.reshape(HALF, 128).astype(BF16), ones) * LOG2E
+
+    def unit(blk, k):
         side, half = blk // 2, blk % 2
-        scores = dot(
-            it[side, pl.ds(pl.multiple_of(half * HALF, HALF), HALF), :], rows[s], 1, 1
-        )
-        t = scores * (LOG2E / scaling_divisor) - lqc[blk]
+        pair = rows[2 * k : 2 * k + 2].reshape(2 * UD, D)
+        scores = dot(it[side, half * HALF : (half + 1) * HALF, :], pair, 1, 1)
+        lift = lqc[blk]
+        t = scores * (LOG2E / scaling_divisor) - jnp.concatenate([lift, lift], axis=1)
         m = jnp.max(t, axis=0, keepdims=True)
         p = jnp.exp2(t - m)
-        mst[blk, pl.ds(s, 1), :] = m
-        lst[blk, pl.ds(s, 1), :] = jnp.sum(p, axis=0, keepdims=True)
+        total = jnp.sum(p, axis=0, keepdims=True)
         p = p.astype(BF16)
-        p_all[blk, :, pl.ds(pl.multiple_of(s * UD, UD), UD)] = p
-        acc[blk, s] = dot(it_t[blk], p)
+        p_all[blk, :, 2 * k * UD : 2 * (k + 1) * UD] = p
+        part = dot(it_t[blk], p)
+        for i in range(2):
+            s, lanes = ORDER[2 * k + i], slice(i * UD, (i + 1) * UD)
+            mst[blk, s : s + 1, :] = m[:, lanes]
+            lst[blk, s : s + 1, :] = total[:, lanes]
+            acc[blk, s] = part[:, lanes]
 
     def wait_users(k):
-        s = offset_of(k)
-        pltpu.make_async_copy(rows.at[0], rows.at[s], z_rs.at[s]).wait()
-
-    def early(blk):
-        def step(k, carry):
-            unit(blk, offset_of(k))
-            return carry
-
-        lax.fori_loop(0, 3, step, 0)
+        pltpu.make_async_copy(rows.at[0], rows.at[k], z_rs.at[k]).wait()
 
     lax.fori_loop(0, 4, arrived, 0)
     c_copy(0).start()
     prepare(0)
-    wait_users(1)
-    wait_users(2)
-    early(0)
+    for k in range(1, 4):
+        wait_users(k)
+    unit(0, 0)
+    unit(0, 1)
     lax.fori_loop(4, 8, arrived, 0)
     c_copy(1).start()
     prepare(1)
-    early(1)
     qc_copy().wait_recv()
     c_copy(0).wait_recv()
     prepare(2)
-    early(2)
+    for blk in (1, 2):
+        unit(blk, 0)
+        unit(blk, 1)
     c_copy(1).wait_recv()
     prepare(3)
-    early(3)
-
-    def late(k, carry):
-        wait_users(k)
-
-        def step(blk, carry):
-            unit(blk, offset_of(k))
-            return carry
-
-        return lax.fori_loop(0, 4, step, carry)
-
-    lax.fori_loop(3, 8, late, 0)
+    unit(3, 0)
+    unit(3, 1)
+    for k in (2, 3):
+        wait_users(2 * k)
+        wait_users(2 * k + 1)
+        for blk in range(4):
+            unit(blk, k)
 
     top = jnp.max(mst[...], axis=0)
     local = top + jnp.log2(sum(lst[k] * jnp.exp2(mst[k] - top) for k in range(4)))
@@ -262,34 +262,23 @@
     share = [jnp.exp2(v[0:1] - lse[0:1]) for v in seen]
     for k in range(4):
         w = jnp.exp2(mst[k] - lse).astype(BF16)
-        for s in range(NZ):
-            w_row[k, :, s * UD : (s + 1) * UD] = w[s : s + 1, :]
-
-    def item_part(blk, c):
-        chunk = pl.ds(pl.multiple_of(c * 128, 128), 128)
-        weights = p_all[blk, chunk, :] * w_row[blk]
-        return dot(weights, rows[...].reshape(NZ * UD, D))
+        for i, s in enumerate(ORDER):
+            w_row[k, :, i * UD : (i + 1) * UD] = w[s : s + 1, :]
+
+    users_all = rows[...].reshape(NZ * UD, D)
+
+    def item_part(blk):
+        return dot(p_all[blk] * w_row[blk], users_all)
 
     def xc_copy(h):
         part = pl.ds(h * HALF, HALF)
         return copy(ip.at[1, part], xc_in.at[part], xc_ss.at[h], xc_rs.at[h], dc=1)
 
     for h in (1, 0):
-        def other(c, carry):
-            spot = pl.ds(pl.multiple_of(h * HALF + c * 128, 128), 128)
-            ip[1, spot, :] = item_part(2 + h, c).astype(BF16)
-            return carry
-
-        lax.fori_loop(0, 4, other, 0)
+        ip[1, h * HALF : (h + 1) * HALF, :] = item_part(2 + h).astype(BF16)
         xc_copy(h).start()
-
     for h in (1, 0):
-        def own(c, carry):
-            spot = pl.ds(pl.multiple_of(h * HALF + c * 128, 128), 128)
-            own_f[spot, :] = item_part(h, c)
-            return carry
-
-        lax.fori_loop(0, 4, own, 0)
+        own_f[h * HALF : (h + 1) * HALF, :] = item_part(h)
 
     def ls_copy(i, j, **to):
         return copy(loss_out.at[i], loss_in.at[j], ls_ss.at[j], ls_rs.at[j], **to)
@@ -363,8 +352,7 @@
     for d in range(1, NY):
         ls_copy(2, 3 + d, dy=d).wait_recv()
         total = total + loss_in[3 + d]
-    users_all = 2 * NX * NY * NZ * UD
-    loss_ref[...] = total[0:1, 0:1] * (1.0 / users_all)
+    loss_ref[...] = total[0:1, 0:1] * (1.0 / (2 * NX * NY * NZ * UD))
 
     for d in range(1, NZ):
         z_copy(d).wait_send()
@@ -408,9 +396,14 @@
             jax.ShapeDtypeStruct((UD, D), F32),
             jax.ShapeDtypeStruct((ID, D), F32),
         ),
-        in_specs=[vmem] * 4,
+        in_specs=[pl.BlockSpec(memory_space=pl.ANY)] * 4,
         out_specs=(vmem,) * 3,
         scratch_shapes=[
+            pltpu.VMEM((UD, D), F32),
+            pltpu.VMEM((ID, D), F32),
+            pltpu.VMEM((1, ID), jnp.int32),
+            pltpu.VMEM((1, UD), jnp.int32),
+            dma(4),
             pltpu.VMEM((NZ, UD, D), BF16),
             pltpu.VMEM((2, 2 * HALF, D), BF16),
             pltpu.VMEM((2, NY, NX, 1, 128), F32),

time: 82 us -> 60.4 us (0.74)
  the two profiles are of different devices: /device:TPU:2 before, /device:TPU:1 now
where the time goes in v2:
time: 60.4 us; the launch traced here: 60.1 us
  Pallas kernels  54.2 us (90%)
  local copies, waits for them, and re-layouts  3.59 us (6%)
  between operations  2.4 us (4%)
    pallas_call x1, Pallas kernels, on_device(): pl.pallas_call(kernel, out_shape=(jax.ShapeDtypeStruct((1, 1), F32), jax....  54.2 us
    unnamed x10, local copies, waits for them, and re-layouts  3.59 us

profile of v2, /device:TPU:1, one launch (start us, length us, event | category | flops | bytes accessed | tf_op | source)
XLA Modules:
  0.0 60.1 jit_solution(204358609198768509)
XLA Ops:
  0.6 0.0 copy-start.2
  0.6 0.0 copy-start.3
  0.7 0.6 %copy-done.2 = s32[32]{0:T(128)S(1)} copy-done((s32[32]{0:T(128)S(1)}, s32[32]{0:T(128)}, u32[]{:S(2)}) %copy-start.2) | copy-done | bytes 152
  1.3 0.0 copy-done.3
  1.3 0.0 copy-start
  1.3 0.9 %copy-done = f32[128,256]{1,0:T(8,128)S(1)} copy-done((f32[128,256]{1,0:T(8,128)S(1)}, f32[128,256]{1,0:T(8,128)}, u32[]{:S(2)}) %copy-start) | copy-done | bytes 131096
  2.2 0.0 copy-start.1
  2.2 0.8 %copy-done.1 = f32[32,256]{1,0:T(8,128)S(1)} copy-done((f32[32,256]{1,0:T(8,128)S(1)}, f32[32,256]{1,0:T(8,128)}, u32[]{:S(2)}) %copy-start.1) | copy-done | bytes 32792
  3.0 54.2 %towers.1 = (f32[1,1]{1,0:T(1,128)}, f32[128,256]{1,0:T(8,128)S(1)}, f32[32,256]{1,0:T(8,128)S(1)}) custom-call(f32[128,256]{1,0:T(8,128)S(1)} %copy-done, f32[32,256]{1,0:T(8,128)S(1)} %copy-done.1, s32[1,32]{1,0:T(1,128)S(1)} %bitcast.3, s32[1,128]{1,0:T(1,128)S(1)} %bitcast.4), custom_call_target="tpu_custom_call" | custom-call | flops 3221225472 | bytes 524288 | tf_op jit(solution)/shard_map/towers/pallas_call | solution.py:392
  57.7 0.7 %copy.11 = f32[128,256]{1,0:T(8,128)} copy(f32[128,256]{1,0:T(8,128)S(1)} %get-tuple-element.13) | data formatting | bytes 262144
  58.4 0.6 %copy.12 = f32[32,256]{1,0:T(8,128)} copy(f32[32,256]{1,0:T(8,128)S(1)} %get-tuple-element.14) | data formatting | bytes 65536
Async XLA Ops:
  0.6 0.7 %copy-start.2 = (s32[32]{0:T(128)S(1)}, s32[32]{0:T(128)}, u32[]{:S(2)}) copy-start(s32[32]{0:T(128)} %param.6) | copy-start | bytes 388
  0.6 0.7 %copy-start.3 = (s32[128]{0:T(128)S(1)}, s32[128]{0:T(128)}, u32[]{:S(2)}) copy-start(s32[128]{0:T(128)} %param.7) | copy-start | bytes 1540
  1.3 0.9 %copy-start = (f32[128,256]{1,0:T(8,128)S(1)}, f32[128,256]{1,0:T(8,128)}, u32[]{:S(2)}) copy-start(f32[128,256]{1,0:T(8,128)} %users_hbm.1) | copy-start | bytes 393220
  2.2 0.8 %copy-start.1 = (f32[32,256]{1,0:T(8,128)S(1)}, f32[32,256]{1,0:T(8,128)}, u32[]{:S(2)}) copy-start(f32[32,256]{1,0:T(8,128)} %items_hbm.1) | copy-start | bytes 98308

commit v3 on v2

--- a/solution.py
+++ b/solution.py
@@ -22,10 +22,6 @@
 HALF = NX * NY * ID // 2
 
 
-def offset_of(k):
-    return jnp.where(k % 2 == 1, (k + 1) // 2, (8 - k // 2) % 8)
-
-
 def dot(a, b, ca=1, cb=0):
     return lax.dot_general(a, b, (((ca,), (cb,)), ((), ())), preferred_element_type=F32)
 
@@ -36,8 +32,7 @@
     users_ref, items_ref, counts_ref, tgt_ref, in_sem,
     rows, it, lq, it_t, lqc, p_all, acc, mst, lst, st_out, st_in, pt_out, pt_in,
     w_row, own_f, ip, xc_in, xs_in, ys_out, ys_in, loss_out, loss_in, tq_s, tv_s,
-    z_ss, z_rs, y_ss, y_rs, ql_ss, ql_rs, x_ss, x_rs, qx_ss, qx_rs, c_ss, c_rs,
-    st_ss, st_rs, pt_ss, pt_rs, xc_ss, xc_rs, xs_ss, xs_rs, ys_ss, ys_rs, ls_ss, ls_rs,
+    sent, z_rs, y_rs, x_rs, c_rs, xc_rs, xs_rs, got,
 ):
     b = lax.axis_index("blk")
     g = lax.axis_index("grp")
@@ -52,6 +47,14 @@
             ((xx // 2) * 8 + (y + dy) % NY) * 2 + (core + dc) % 2,
             ((z + dz) % NZ) * 2 + xx % 2,
         )
+
+    Z_S, Y_S, QL_S, X_S, QX_S, C_S, QC_S, ST_S, PT_S, XC_S, XS_S, YS_S, L0_S, L1_S, L2_S = (
+        sent.at[k] for k in range(15)
+    )
+    QL_R, QX_R, QC_R, ST_R, PT_R, YS_R, L0_R, L1_R, L2_R = (got.at[k] for k in range(9))
+
+    def whole(ref, sem):
+        pltpu.make_async_copy(ref, ref, sem).wait()
 
     def copy(src, dst, ss, rs, **to):
         return pltpu.make_async_remote_copy(
@@ -88,41 +91,56 @@
 
     def z_copy(d):
         s = SLOT[(NZ - d) % NZ]
-        return copy(rows.at[0], rows.at[s], z_ss.at[d], z_rs.at[s], dz=d)
+        return copy(rows.at[0], rows.at[s], Z_S, z_rs.at[s // 2], dz=d)
 
     def y_copy(d):
         s = SLOT[(NY - d) % NY]
         return copy(
-            it.at[0, pl.ds(0, ID)], it.at[0, pl.ds(s * NX * ID, ID)], y_ss.at[d], y_rs.at[s], dy=d
+            it.at[0, pl.ds(0, ID)], it.at[0, pl.ds(s * NX * ID, ID)], Y_S, y_rs.at[s], dy=d
         )
 
     def ql_copy(d):
         s = SLOT[(NY - d) % NY]
-        return copy(lq.at[0, 0, 0], lq.at[0, s, 0], ql_ss.at[d], ql_rs.at[s], dy=d)
+        return copy(lq.at[0, 0, 0], lq.at[0, s, 0], QL_S, QL_R, dy=d)
 
     def x_copy(s, e):
         return copy(
             it.at[0, pl.ds(s * NX * ID, ID)],
             it.at[0, pl.ds((s * NX + NX - e) * ID, ID)],
-            x_ss.at[s, e], x_rs.at[s, NX - e], dx=e,
+            X_S, x_rs.at[s], dx=e,
         )
 
     def qx_copy(e):
-        return copy(lq.at[0, :, 0], lq.at[0, :, NX - e], qx_ss.at[e], qx_rs.at[NX - e], dx=e)
-
-    def c_copy(h):
-        part = pl.ds(h * HALF, HALF)
-        return copy(it.at[0, part], it.at[1, part], c_ss.at[h], c_rs.at[h], dc=1)
+        return copy(lq.at[0, :, 0], lq.at[0, :, NX - e], QX_S, QX_R, dx=e)
+
+    def c_copy(s):
+        part = pl.ds(s * NX * ID, NX * ID)
+        return copy(it.at[0, part], it.at[1, part], C_S, c_rs.at[s // 4], dc=1)
 
     def qc_copy():
-        return copy(lq.at[0], lq.at[1], c_ss.at[2], c_rs.at[2], dc=1)
+        return copy(lq.at[0], lq.at[1], QC_S, QC_R, dc=1)
 
     for d in ORDER[1:]:
         ql_copy(d).start()
+    for d in ORDER[1:]:
         y_copy(d).start()
-        z_copy(d).start()
     for e in range(1, NX):
         x_copy(0, e).start()
+    for d in ORDER[1:]:
+        z_copy(d).start()
+
+    def forward(s):
+        whole(it.at[0, pl.ds(s * NX * ID, ID)], y_rs.at[s])
+        for e in range(1, NX):
+            x_copy(s, e).start()
+
+    for s in range(1, 4):
+        forward(s)
+    whole(lq.at[0, 1:NY, 0], QL_R)
+    for e in range(1, NX):
+        qx_copy(e).start()
+    for s in range(4, 8):
+        forward(s)
 
     first = (b * 16 + g) * ID
     hot = (
@@ -146,29 +164,9 @@
     )
     st_out[1] = jnp.broadcast_to(pos, (8, 128))
 
-    def forward(s, carry):
-        pltpu.make_async_copy(
-            it.at[0, pl.ds(0, ID)], it.at[0, pl.ds(s * NX * ID, ID)], y_rs.at[s]
-        ).wait()
-        for e in range(1, NX):
-            x_copy(s, e).start()
-        return carry
-
-    lax.fori_loop(1, 4, forward, 0)
-    for s in range(1, NY):
-        pltpu.make_async_copy(lq.at[0, 0, 0], lq.at[0, s, 0], ql_rs.at[s]).wait()
-    for e in range(1, NX):
-        qx_copy(e).start()
-    lax.fori_loop(4, 8, forward, 0)
-    for e in range(1, NX):
-        pltpu.make_async_copy(lq.at[0, :, 0], lq.at[0, :, e], qx_rs.at[e]).wait()
-    qc_copy().start()
-
-    def arrived(s, carry):
-        for e in range(1, NX):
-            spot = it.at[0, pl.ds((s * NX + e) * ID, ID)]
-            pltpu.make_async_copy(spot, spot, x_rs.at[s, e]).wait()
-        return carry
+    def arrived(s):
+        whole(it.at[0, pl.ds((s * NX + 1) * ID, 3 * ID)], x_rs.at[s])
+        c_copy(s).start()
 
     ones = jnp.ones((128, 128), BF16)
 
@@ -198,31 +196,32 @@
             acc[blk, s] = part[:, lanes]
 
     def wait_users(k):
-        pltpu.make_async_copy(rows.at[0], rows.at[k], z_rs.at[k]).wait()
-
-    lax.fori_loop(0, 4, arrived, 0)
-    c_copy(0).start()
+        whole(rows.at[max(2 * k, 1) : 2 * k + 2], z_rs.at[k])
+
+    for s in range(4):
+        arrived(s)
+    whole(lq.at[0, :, 1:NX], QX_R)
+    qc_copy().start()
     prepare(0)
-    for k in range(1, 4):
-        wait_users(k)
+    wait_users(0)
+    wait_users(1)
     unit(0, 0)
     unit(0, 1)
-    lax.fori_loop(4, 8, arrived, 0)
-    c_copy(1).start()
+    for s in range(4, 8):
+        arrived(s)
+    qc_copy().wait_recv()
+    whole(it.at[1, pl.ds(0, HALF)], c_rs.at[0])
     prepare(1)
-    qc_copy().wait_recv()
-    c_copy(0).wait_recv()
     prepare(2)
     for blk in (1, 2):
         unit(blk, 0)
         unit(blk, 1)
-    c_copy(1).wait_recv()
+    whole(it.at[1, pl.ds(HALF, HALF)], c_rs.at[1])
     prepare(3)
     unit(3, 0)
     unit(3, 1)
     for k in (2, 3):
-        wait_users(2 * k)
-        wait_users(2 * k + 1)
+        wait_users(k)
         for blk in range(4):
             unit(blk, k)
 
@@ -231,12 +230,10 @@
     st_out[0] = local
 
     def st_copy(d):
-        return copy(st_out, st_in.at[(NZ - d) % NZ], st_ss.at[d], st_rs.at[(NZ - d) % NZ], dz=d)
+        return copy(st_out, st_in.at[(NZ - d) % NZ], ST_S, ST_R, dz=d)
 
     def pt_copy(d):
-        return copy(
-            pt_out.at[d], pt_in.at[(NZ - d) % NZ], pt_ss.at[d], pt_rs.at[(NZ - d) % NZ], dz=d
-        )
+        return copy(pt_out.at[d], pt_in.at[(NZ - d) % NZ], PT_S, PT_R, dz=d)
 
     for d in (4, 3, 5, 2, 6, 1, 7):
         st_copy(d).start()
@@ -254,8 +251,15 @@
 
     lax.fori_loop(1, NZ, give, 0)
 
-    for e in range(1, NZ):
-        pltpu.make_async_copy(st_out, st_in.at[e], st_rs.at[e]).wait()
+    whole(rows.at[1:NZ], Z_S)
+    whole(it.at[0, pl.ds(0, 7 * ID)], Y_S)
+    whole(lq.at[0, 1:NY, 0], QL_S)
+    whole(it.at[0, pl.ds(0, 24 * ID)], X_S)
+    whole(lq.at[0, :, 1:NX], QX_S)
+    whole(it.at[0], C_S)
+    whole(lq.at[0], QC_S)
+
+    whole(st_in.at[1:NZ], ST_R)
     seen = [local] + [jnp.roll(st_in[e, 0], e, axis=0) for e in range(1, NZ)]
     top = functools.reduce(jnp.maximum, seen)
     lse = top + jnp.log2(sum(jnp.exp2(v - top) for v in seen))
@@ -272,7 +276,7 @@
 
     def xc_copy(h):
         part = pl.ds(h * HALF, HALF)
-        return copy(ip.at[1, part], xc_in.at[part], xc_ss.at[h], xc_rs.at[h], dc=1)
+        return copy(ip.at[1, part], xc_in.at[part], XC_S, xc_rs.at[h], dc=1)
 
     for h in (1, 0):
         ip[1, h * HALF : (h + 1) * HALF, :] = item_part(2 + h).astype(BF16)
@@ -281,7 +285,8 @@
         own_f[h * HALF : (h + 1) * HALF, :] = item_part(h)
 
     def ls_copy(i, j, **to):
-        return copy(loss_out.at[i], loss_in.at[j], ls_ss.at[j], ls_rs.at[j], **to)
+        ss, rs = ((L0_S, L0_R), (L1_S, L1_R), (L2_S, L2_R))[i]
+        return copy(loss_out.at[i], loss_in.at[j], ss, rs, **to)
 
     pos_all = st_out[1] + sum(st_in[e, 1] for e in range(1, NZ))
     line = jnp.sum(jnp.sum(lse, axis=1, keepdims=True), axis=0, keepdims=True) * LN2
@@ -291,103 +296,72 @@
     def xs_copy(s, e):
         return copy(
             ip.at[0, pl.ds((s * NX + e) * ID, ID)], xs_in.at[s, NX - e],
-            xs_ss.at[s, e], xs_rs.at[s, NX - e], dx=e,
+            XS_S, xs_rs.at[s], dx=e,
         )
 
     for h in (1, 0):
         xc_copy(h).wait_recv()
-
-        def own_sum(s, carry):
-            spot = pl.ds(pl.multiple_of(s * NX * ID, NX * ID), NX * ID)
+        for k in range(h * 4 + 3, h * 4 - 1, -1):
+            spot = slice(k * NX * ID, (k + 1) * NX * ID)
             total = own_f[spot, :] + xc_in[spot, :].astype(F32)
             own_f[spot, :] = total
             ip[0, spot, :] = total.astype(BF16)
             for e in (2, 1, 3):
-                xs_copy(s, e).start()
-            return carry
-
-        lax.fori_loop(h * 4, h * 4 + 4, own_sum, 0)
-
-    ls_copy(0, 0, dc=1).wait_recv()
+                xs_copy(k, e).start()
+
+    whole(loss_in.at[0], L0_R)
     loss_out[1] = loss_out[0] + loss_in[0]
     for e in range(1, NX):
         ls_copy(1, e, dx=e).start()
 
     def ys_copy(s):
-        o = offset_of(s)
-        mirror = jnp.where(s == 0, 0, jnp.where(s == 7, 7, jnp.where(s % 2 == 1, s + 1, s - 1)))
-        return copy(ys_out.at[s], ys_in.at[mirror], ys_ss.at[s], ys_rs.at[mirror], dy=o)
+        mirror = SLOT[(NY - ORDER[s]) % NY]
+        return copy(
+            ys_out.at[s], ys_in.at[mirror], YS_S, YS_R, dy=ORDER[s]
+        )
 
     def x_total(s):
-        for e in range(1, NX):
-            pltpu.make_async_copy(xs_in.at[s, e], xs_in.at[s, e], xs_rs.at[s, e]).wait()
-        spot = pl.ds(pl.multiple_of(s * NX * ID, NX * ID), ID)
+        whole(xs_in.at[s, 1:NX], xs_rs.at[s])
+        spot = slice(s * NX * ID, s * NX * ID + ID)
         return own_f[spot, :] + sum(xs_in[s, e].astype(F32) for e in range(1, NX))
 
-    def relay(i, carry):
-        s = 7 - i
+    for s in range(NY - 1, 0, -1):
         ys_out[s] = x_total(s).astype(BF16)
         ys_copy(s).start()
-        return carry
-
-    lax.fori_loop(0, 7, relay, 0)
-    for e in range(1, NX):
-        ls_copy(1, e, dx=e).wait_recv()
+    whole(loss_in.at[1:NX], L1_R)
     loss_out[2] = loss_out[1] + loss_in[1] + loss_in[2] + loss_in[3]
     for d in range(1, NY):
         ls_copy(2, 3 + d, dy=d).start()
     cand = x_total(0) - tq_s[...]
 
     user_sum = part_of(0) * share[0] - tv_s[...]
+    whole(pt_in.at[1:NZ], PT_R)
     for e in range(1, NZ):
-        pltpu.make_async_copy(pt_in.at[e], pt_in.at[e], pt_rs.at[e]).wait()
         user_sum = user_sum + pt_in[e].astype(F32) * share[e]
     query_ref[...] = user_sum.T * (1.0 / scaling_divisor)
-
+    whole(st_in.at[1:NZ], ST_S)
+    whole(pt_in.at[1:NZ], PT_S)
+    whole(ip.at[1], XC_S)
+    whole(xs_in.at[:, 1:NX], XS_S)
+    whole(loss_in.at[0], L0_S)
+    whole(loss_in.at[1:NX], L1_S)
+
+    whole(ys_in.at[1:NY], YS_R)
     for s in range(1, NY):
-        pltpu.make_async_copy(ys_in.at[s], ys_in.at[s], ys_rs.at[s]).wait()
         cand = cand + ys_in[s].astype(F32)
     cand_ref[...] = cand * (1.0 / scaling_divisor)
     total = loss_out[2]
+    whole(loss_in.at[4:11], L2_R)
     for d in range(1, NY):
-        ls_copy(2, 3 + d, dy=d).wait_recv()
         total = total + loss_in[3 + d]
     loss_ref[...] = total[0:1, 0:1] * (1.0 / (2 * NX * NY * NZ * UD))
 
-    for d in range(1, NZ):
-        z_copy(d).wait_send()
-        y_copy(d).wait_send()
-        ql_copy(d).wait_send()
-        st_copy(d).wait_send()
-        pt_copy(d).wait_send()
-        ls_copy(2, 3 + d, dy=d).wait_send()
-    for e in range(1, NX):
-        qx_copy(e).wait_send()
-        ls_copy(1, e, dx=e).wait_send()
-
-    def left(s, carry):
-        for e in range(1, NX):
-            x_copy(s, e).wait_send()
-            xs_copy(s, e).wait_send()
-        return carry
-
-    lax.fori_loop(0, NY, left, 0)
-
-    def left_y(s, carry):
-        ys_copy(s).wait_send()
-        return carry
-
-    lax.fori_loop(1, NY, left_y, 0)
-    for h in range(2):
-        c_copy(h).wait_send()
-        xc_copy(h).wait_send()
-    qc_copy().wait_send()
-    ls_copy(0, 0, dc=1).wait_send()
+    whole(ys_in.at[1:NY], YS_S)
+    whole(loss_in.at[4:11], L2_S)
 
 
 def on_device(users, items, counts, target_indices):
     dma = lambda *n: pltpu.SemaphoreType.DMA(n)
-    pair = lambda *n: [dma(*n), dma(*n)]
     vmem = pl.BlockSpec(memory_space=pltpu.VMEM)
     loss, query, cand = pl.pallas_call(
         kernel,
@@ -396,7 +370,7 @@
             jax.ShapeDtypeStruct((UD, D), F32),
             jax.ShapeDtypeStruct((ID, D), F32),
         ),
-        in_specs=[pl.BlockSpec(memory_space=pl.ANY)] * 4,
+        in_specs=[pl.BlockSpec(memory_space=pltpu.HBM)] * 4,
         out_specs=(vmem,) * 3,
         scratch_shapes=[
             pltpu.VMEM((UD, D), F32),
@@ -428,11 +402,10 @@
             pltpu.VMEM((11, 8, 128), F32),
             pltpu.VMEM((ID, D), F32),
             pltpu.VMEM((D, UD), F32),
-            *pair(NZ), *pair(NY), *pair(NY), *pair(NY, NX), *pair(NX), *pair(3),
-            *pair(NZ), *pair(NZ), *pair(2), *pair(NY, NX), *pair(NY), *pair(11),
+            dma(15), dma(NZ // 2), dma(NY), dma(NY), dma(2), dma(2), dma(NY), dma(9),
         ],
         compiler_params=pltpu.CompilerParams(
-            collective_id=0, has_side_effects=True, vmem_limit_bytes=48 * 2**20
+            collective_id=0, has_side_effects=True, vmem_limit_bytes=64 * 2**20
         ),
         cost_estimate=pl.CostEstimate(
             flops=6 * 1024 * 2048 * D, bytes_accessed=2**19, transcendentals=1024 * 2048

time: 60.4 us -> 57.4 us (0.950)
  Pallas kernels: 54.2 us -> 52.6 us
  local copies, waits for them, and re-layouts: 3.59 us -> 2.19 us
    pallas_call x1, Pallas kernels: 54.2 us -> 52.6 us  [on_device(): pl.pallas_call(kernel, out_shape=(jax.ShapeDtypeStruct((1, 1), F32), jax....]
    unnamed x10 -> x4, local copies, waits for them, and re-layouts: 3.59 us -> 2.19 us
where the time goes in v3:
time: 57.4 us; the launch traced here: 57.2 us
  Pallas kernels  52.6 us (92%)
  between operations  2.4 us (4%)
  local copies, waits for them, and re-layouts  2.19 us (4%)
    pallas_call x1, Pallas kernels, on_device(): pl.pallas_call(kernel, out_shape=(jax.ShapeDtypeStruct((1, 1), F32), jax....  52.6 us
    unnamed x4, local copies, waits for them, and re-layouts  2.19 us

profile of v3, /device:TPU:1, one launch (start us, length us, event | category | flops | bytes accessed | tf_op | source)
XLA Modules:
  0.0 57.2 jit_solution(17152302831607920953)
XLA Ops:
  0.6 52.6 %towers.1 = (f32[1,1]{1,0:T(1,128)}, f32[128,256]{1,0:T(8,128)}, f32[32,256]{1,0:T(8,128)}) custom-call(f32[128,256]{1,0:T(8,128)} %users_hbm.1, f32[32,256]{1,0:T(8,128)} %items_hbm.1, s32[1,32]{1,0:T(1,128)} %bitcast.3, s32[1,128]{1,0:T(1,128)} %bitcast.4), custom_call_target="tpu_custom_call" | custom-call | flops 3221225472 | bytes 524288 | tf_op jit(solution)/shard_map/towers/pallas_call | solution.py:366
  53.9 0.0 copy-start
  53.9 1.6 %copy.11 = f32[128,256]{1,0:T(8,128)} copy(f32[128,256]{1,0:T(8,128)} %get-tuple-element.13) | data formatting | bytes 262144
  55.5 0.0 copy-done
  55.5 0.6 %copy.12 = f32[32,256]{1,0:T(8,128)} copy(f32[32,256]{1,0:T(8,128)S(1)} %copy-done) | data formatting | bytes 65536
Async XLA Ops:
  53.9 1.6 %copy-start = (f32[32,256]{1,0:T(8,128)S(1)}, f32[32,256]{1,0:T(8,128)}, u32[]{:S(2)}) copy-start(f32[32,256]{1,0:T(8,128)} %get-tuple-element.14) | copy-start | bytes 98308

commit v4 on v3

--- a/solution.py
+++ b/solution.py
@@ -20,6 +20,8 @@
 ORDER = (0, 1, 7, 2, 6, 3, 5, 4)
 SLOT = tuple(ORDER.index(k) for k in range(NY))
 HALF = NX * NY * ID // 2
+BLOCKS = tuple((i, r, n) for i in range(2) for r, n in ((0, 512), (512, 256), (768, 256)))
+NB = len(BLOCKS)
 
 
 def dot(a, b, ca=1, cb=0):
@@ -28,11 +30,12 @@
 
 def kernel(
     users_hbm, items_hbm, counts_hbm, tgt_hbm,
-    loss_ref, query_ref, cand_ref,
+    loss_ref, query_hbm, cand_hbm,
+    query_ref, cand_ref,
     users_ref, items_ref, counts_ref, tgt_ref, in_sem,
     rows, it, lq, it_t, lqc, p_all, acc, mst, lst, st_out, st_in, pt_out, pt_in,
     w_row, own_f, ip, xc_in, xs_in, ys_out, ys_in, loss_out, loss_in, tq_s, tv_s,
-    sent, z_rs, y_rs, x_rs, c_rs, xc_rs, xs_rs, got,
+    sent, z_rs, y_rs, x_rs, c_rs, xc_rs, xs_rs, got, out_sem,
 ):
     b = lax.axis_index("blk")
     g = lax.axis_index("grp")
@@ -61,6 +64,15 @@
             src_ref=src, dst_ref=dst, send_sem=ss, recv_sem=rs,
             device_id=device(**to), device_id_type=MESH,
         )
+
+    loads = [
+        pltpu.make_async_copy(src, dst, in_sem.at[k])
+        for k, (src, dst) in enumerate((
+            (counts_hbm, counts_ref), (items_hbm, items_ref), (users_hbm, users_ref), (tgt_hbm, tgt_ref)
+        ))
+    ]
+    for load in loads:
+        load.start()
 
     barrier = pltpu.get_barrier_semaphore()
     for d in range(1, NZ):
@@ -71,17 +83,8 @@
         pl.semaphore_signal(barrier, inc=1, device_id=device(dx=d), device_id_type=MESH)
     pl.semaphore_signal(barrier, inc=1, device_id=device(dc=1), device_id_type=MESH)
 
-    loads = [
-        pltpu.make_async_copy(src, dst, in_sem.at[k])
-        for k, (src, dst) in enumerate((
-            (counts_hbm, counts_ref), (items_hbm, items_ref), (users_hbm, users_ref), (tgt_hbm, tgt_ref)
-        ))
-    ]
-    for load in loads:
-        load.start()
-    for load in loads:
-        load.wait()
-    rows[0] = users_ref[...].astype(BF16)
+    loads[0].wait()
+    loads[1].wait()
     it[0, 0:ID, :] = items_ref[...].astype(BF16)
     logq = jnp.log(counts_ref[...].astype(F32)).astype(BF16).astype(F32)
     logq = jnp.concatenate([logq, jnp.zeros((1, 128 - ID), F32)], axis=1)
@@ -115,17 +118,19 @@
 
     def c_copy(s):
         part = pl.ds(s * NX * ID, NX * ID)
-        return copy(it.at[0, part], it.at[1, part], C_S, c_rs.at[s // 4], dc=1)
+        return copy(it.at[0, part], it.at[1, part], C_S, c_rs.at[max(s // 2 - 1, 0)], dc=1)
 
     def qc_copy():
         return copy(lq.at[0], lq.at[1], QC_S, QC_R, dc=1)
 
-    for d in ORDER[1:]:
+    for d in (4, 1, 7, 3, 5, 2, 6):
+        y_copy(d).start()
+    for d in (4, 1, 7, 3, 5, 2, 6):
         ql_copy(d).start()
-    for d in ORDER[1:]:
-        y_copy(d).start()
     for e in range(1, NX):
         x_copy(0, e).start()
+    loads[2].wait()
+    rows[0] = users_ref[...].astype(BF16)
     for d in ORDER[1:]:
         z_copy(d).start()
 
@@ -143,6 +148,7 @@
         forward(s)
 
     first = (b * 16 + g) * ID
+    loads[3].wait()
     hot = (
         lax.broadcasted_iota(jnp.int32, (ID, UD), 0) + first == tgt_ref[...]
     ).astype(F32)
@@ -170,33 +176,45 @@
 
     ones = jnp.ones((128, 128), BF16)
 
+    def spot_of(blk):
+        side, row, n = BLOCKS[blk]
+        return slice(side * 2 * HALF + row, side * 2 * HALF + row + n)
+
     def prepare(blk):
-        side, half = blk // 2, blk % 2
-        it_t[blk] = it[side, half * HALF : (half + 1) * HALF, :].T
-        row = lq[side, half * 4 : (half + 1) * 4].reshape(16, 1, 128)
-        spread = jnp.where(eye[None], jnp.broadcast_to(row, (16, ID, 128)), 0.0)
-        lqc[blk] = dot(spread.reshape(HALF, 128).astype(BF16), ones) * LOG2E
+        side, row, n = BLOCKS[blk]
+        it_t[:, spot_of(blk)] = it[side, row : row + n, :].T
+        shards = n // ID
+        first_slot = row // (NX * ID)
+        found = lq[side, first_slot : first_slot + shards // NX].reshape(shards, 1, 128)
+        spread = jnp.where(eye[None], jnp.broadcast_to(found, (shards, ID, 128)), 0.0)
+        lqc[spot_of(blk), :] = dot(spread.reshape(n, 128).astype(BF16), ones) * LOG2E
 
     def unit(blk, k):
-        side, half = blk // 2, blk % 2
+        side, row, n = BLOCKS[blk]
         pair = rows[2 * k : 2 * k + 2].reshape(2 * UD, D)
-        scores = dot(it[side, half * HALF : (half + 1) * HALF, :], pair, 1, 1)
-        lift = lqc[blk]
+        scores = dot(it[side, row : row + n, :], pair, 1, 1)
+        lift = lqc[spot_of(blk), :]
         t = scores * (LOG2E / scaling_divisor) - jnp.concatenate([lift, lift], axis=1)
         m = jnp.max(t, axis=0, keepdims=True)
         p = jnp.exp2(t - m)
         total = jnp.sum(p, axis=0, keepdims=True)
-        p = p.astype(BF16)
-        p_all[blk, :, 2 * k * UD : 2 * (k + 1) * UD] = p
-        part = dot(it_t[blk], p)
+        p_all[spot_of(blk), 2 * k * UD : 2 * (k + 1) * UD] = p.astype(BF16)
         for i in range(2):
             s, lanes = ORDER[2 * k + i], slice(i * UD, (i + 1) * UD)
             mst[blk, s : s + 1, :] = m[:, lanes]
             lst[blk, s : s + 1, :] = total[:, lanes]
-            acc[blk, s] = part[:, lanes]
+
+    def weighted(blk, k):
+        part = dot(it_t[:, spot_of(blk)], p_all[spot_of(blk), 2 * k * UD : 2 * (k + 1) * UD])
+        for i in range(2):
+            acc[blk, ORDER[2 * k + i]] = part[:, i * UD : (i + 1) * UD]
 
     def wait_users(k):
         whole(rows.at[max(2 * k, 1) : 2 * k + 2], z_rs.at[k])
+
+    def wait_other(k):
+        row, n = ((0, 512), (512, 256), (768, 256))[k]
+        whole(it.at[1, pl.ds(row, n)], c_rs.at[k])
 
     for s in range(4):
         arrived(s)
@@ -207,26 +225,32 @@
     wait_users(1)
     unit(0, 0)
     unit(0, 1)
-    for s in range(4, 8):
-        arrived(s)
+    arrived(4)
+    arrived(5)
     qc_copy().wait_recv()
-    whole(it.at[1, pl.ds(0, HALF)], c_rs.at[0])
+    wait_other(0)
     prepare(1)
-    prepare(2)
-    for blk in (1, 2):
+    prepare(3)
+    for blk in (1, 3):
         unit(blk, 0)
         unit(blk, 1)
-    whole(it.at[1, pl.ds(HALF, HALF)], c_rs.at[1])
-    prepare(3)
-    unit(3, 0)
-    unit(3, 1)
+    arrived(6)
+    arrived(7)
+    prepare(2)
+    unit(2, 0)
+    unit(2, 1)
     for k in (2, 3):
         wait_users(k)
         for blk in range(4):
             unit(blk, k)
+    for blk in (4, 5):
+        wait_other(blk - 3)
+        prepare(blk)
+        for k in range(4):
+            unit(blk, k)
 
     top = jnp.max(mst[...], axis=0)
-    local = top + jnp.log2(sum(lst[k] * jnp.exp2(mst[k] - top) for k in range(4)))
+    local = top + jnp.log2(sum(lst[k] * jnp.exp2(mst[k] - top) for k in range(NB)))
     st_out[0] = local
 
     def st_copy(d):
@@ -238,11 +262,14 @@
     for d in (4, 3, 5, 2, 6, 1, 7):
         st_copy(d).start()
 
-    for k in range(4):
+    for k in range(NB):
         lst[k] = jnp.exp2(mst[k] - local)
+    for k in (3, 2, 1, 0):
+        for blk in range(NB):
+            weighted(blk, k)
 
     def part_of(s):
-        return sum(acc[k, s] * lst[k, pl.ds(s, 1), :] for k in range(4))
+        return sum(acc[k, s] * lst[k, pl.ds(s, 1), :] for k in range(NB))
 
     def give(s, carry):
         pt_out[s] = part_of(s).astype(BF16)
@@ -264,25 +291,28 @@
     top = functools.reduce(jnp.maximum, seen)
     lse = top + jnp.log2(sum(jnp.exp2(v - top) for v in seen))
     share = [jnp.exp2(v[0:1] - lse[0:1]) for v in seen]
-    for k in range(4):
+    for k in range(NB):
         w = jnp.exp2(mst[k] - lse).astype(BF16)
         for i, s in enumerate(ORDER):
             w_row[k, :, i * UD : (i + 1) * UD] = w[s : s + 1, :]
 
     users_all = rows[...].reshape(NZ * UD, D)
 
-    def item_part(blk):
-        return dot(p_all[blk] * w_row[blk], users_all)
-
-    def xc_copy(h):
-        part = pl.ds(h * HALF, HALF)
-        return copy(ip.at[1, part], xc_in.at[part], XC_S, xc_rs.at[h], dc=1)
-
-    for h in (1, 0):
-        ip[1, h * HALF : (h + 1) * HALF, :] = item_part(2 + h).astype(BF16)
-        xc_copy(h).start()
-    for h in (1, 0):
-        own_f[h * HALF : (h + 1) * HALF, :] = item_part(h)
+    def item_part(blk, row, n):
+        return dot(p_all[row : row + n, :] * w_row[blk], users_all)
+
+    QUARTER = HALF // 2
+
+    def xc_copy(c):
+        part = pl.ds(c * QUARTER, QUARTER)
+        return copy(ip.at[1, part], xc_in.at[part], XC_S, xc_rs.at[c], dc=1)
+
+    for c, blk in ((3, 5), (2, 4), (1, 3), (0, 3)):
+        part = item_part(blk, 2 * HALF + c * QUARTER, QUARTER)
+        ip[1, c * QUARTER : (c + 1) * QUARTER, :] = part.astype(BF16)
+        xc_copy(c).start()
+    for blk in (2, 1, 0):
+        own_f[spot_of(blk), :] = item_part(blk, BLOCKS[blk][1], BLOCKS[blk][2])
 
     def ls_copy(i, j, **to):
         ss, rs = ((L0_S, L0_R), (L1_S, L1_R), (L2_S, L2_R))[i]
@@ -299,9 +329,9 @@
             XS_S, xs_rs.at[s], dx=e,
         )
 
-    for h in (1, 0):
-        xc_copy(h).wait_recv()
-        for k in range(h * 4 + 3, h * 4 - 1, -1):
+    for c in (3, 2, 1, 0):
+        xc_copy(c).wait_recv()
+        for k in (2 * c + 1, 2 * c):
             spot = slice(k * NX * ID, (k + 1) * NX * ID)
             total = own_f[spot, :] + xc_in[spot, :].astype(F32)
             own_f[spot, :] = total
@@ -339,6 +369,8 @@
     for e in range(1, NZ):
         user_sum = user_sum + pt_in[e].astype(F32) * share[e]
     query_ref[...] = user_sum.T * (1.0 / scaling_divisor)
+    query_out = pltpu.make_async_copy(query_ref, query_hbm, out_sem.at[0])
+    query_out.start()
     whole(st_in.at[1:NZ], ST_S)
     whole(pt_in.at[1:NZ], PT_S)
     whole(ip.at[1], XC_S)
@@ -350,6 +382,8 @@
     for s in range(1, NY):
         cand = cand + ys_in[s].astype(F32)
     cand_ref[...] = cand * (1.0 / scaling_divisor)
+    cand_out = pltpu.make_async_copy(cand_ref, cand_hbm, out_sem.at[1])
+    cand_out.start()
     total = loss_out[2]
     whole(loss_in.at[4:11], L2_R)
     for d in range(1, NY):
@@ -358,21 +392,47 @@
 
     whole(ys_in.at[1:NY], YS_S)
     whole(loss_in.at[4:11], L2_S)
+    query_out.wait()
+    cand_out.wait()
+
+
+def settle(
+    loss_in, query_in, cand_in, loss_out, query_out, cand_out, query_v, cand_v, in_sem, out_sem
+):
+    ins = [
+        pltpu.make_async_copy(query_in, query_v, in_sem.at[0]),
+        pltpu.make_async_copy(cand_in, cand_v, in_sem.at[1]),
+    ]
+    outs = [
+        pltpu.make_async_copy(query_v, query_out, out_sem.at[0]),
+        pltpu.make_async_copy(cand_v, cand_out, out_sem.at[1]),
+    ]
+    for move in ins:
+        move.start()
+    loss_out[...] = loss_in[...]
+    for arrival, departure in zip(ins, outs):
+        arrival.wait()
+        departure.start()
+    for departure in outs:
+        departure.wait()
 
 
 def on_device(users, items, counts, target_indices):
     dma = lambda *n: pltpu.SemaphoreType.DMA(n)
-    vmem = pl.BlockSpec(memory_space=pltpu.VMEM)
-    loss, query, cand = pl.pallas_call(
+    anywhere = pl.BlockSpec(memory_space=pl.ANY)
+    results = (
+        jax.ShapeDtypeStruct((1, 1), F32),
+        jax.ShapeDtypeStruct((UD, D), F32),
+        jax.ShapeDtypeStruct((ID, D), F32),
+    )
+    found = pl.pallas_call(
         kernel,
-        out_shape=(
-            jax.ShapeDtypeStruct((1, 1), F32),
-            jax.ShapeDtypeStruct((UD, D), F32),
-            jax.ShapeDtypeStruct((ID, D), F32),
-        ),
-        in_specs=[pl.BlockSpec(memory_space=pltpu.HBM)] * 4,
-        out_specs=(vmem,) * 3,
+        out_shape=results,
+        in_specs=[anywhere] * 4,
+        out_specs=(pl.BlockSpec(memory_space=pltpu.VMEM), anywhere, anywhere),
         scratch_shapes=[
+            pltpu.VMEM((UD, D), F32),
+            pltpu.VMEM((ID, D), F32),
             pltpu.VMEM((UD, D), F32),
             pltpu.VMEM((ID, D), F32),
             pltpu.VMEM((1, ID), jnp.int32),
@@ -381,17 +441,17 @@
             pltpu.VMEM((NZ, UD, D), BF16),
             pltpu.VMEM((2, 2 * HALF, D), BF16),
             pltpu.VMEM((2, NY, NX, 1, 128), F32),
-            pltpu.VMEM((4, D, HALF), BF16),
-            pltpu.VMEM((4, HALF, 128), F32),
-            pltpu.VMEM((4, HALF, NZ * UD), BF16),
-            pltpu.VMEM((4, NZ, D, UD), F32),
-            pltpu.VMEM((4, NZ, UD), F32),
-            pltpu.VMEM((4, NZ, UD), F32),
+            pltpu.VMEM((D, 4 * HALF), BF16),
+            pltpu.VMEM((4 * HALF, 128), F32),
+            pltpu.VMEM((4 * HALF, NZ * UD), BF16),
+            pltpu.VMEM((NB, NZ, D, UD), F32),
+            pltpu.VMEM((NB, NZ, UD), F32),
+            pltpu.VMEM((NB, NZ, UD), F32),
             pltpu.VMEM((2, 8, 128), F32),
             pltpu.VMEM((NZ, 2, 8, 128), F32),
             pltpu.VMEM((NZ, D, UD), BF16),
             pltpu.VMEM((NZ, D, UD), BF16),
-            pltpu.VMEM((4, 1, NZ * UD), BF16),
+            pltpu.VMEM((NB, 1, NZ * UD), BF16),
             pltpu.VMEM((2 * HALF, D), F32),
             pltpu.VMEM((2, 2 * HALF, D), BF16),
             pltpu.VMEM((2 * HALF, D), BF16),
@@ -402,7 +462,7 @@
             pltpu.VMEM((11, 8, 128), F32),
             pltpu.VMEM((ID, D), F32),
             pltpu.VMEM((D, UD), F32),
-            dma(15), dma(NZ // 2), dma(NY), dma(NY), dma(2), dma(2), dma(NY), dma(9),
+            dma(15), dma(NZ // 2), dma(NY), dma(NY), dma(3), dma(4), dma(NY), dma(9), dma(2),
         ],
         compiler_params=pltpu.CompilerParams(
             collective_id=0, has_side_effects=True, vmem_limit_bytes=64 * 2**20
@@ -412,6 +472,16 @@
         ),
         name="towers",
     )(users, items, counts.reshape(1, ID), target_indices.reshape(1, UD))
+    small = pl.BlockSpec(memory_space=pltpu.VMEM)
+    loss, query, cand = pl.pallas_call(
+        settle,
+        out_shape=results,
+        in_specs=[small, anywhere, anywhere],
+        out_specs=(small, anywhere, anywhere),
+        scratch_shapes=[pltpu.VMEM((UD, D), F32), pltpu.VMEM((ID, D), F32), dma(2), dma(2)],
+        compiler_params=pltpu.CompilerParams(vmem_limit_bytes=64 * 2**20),
+        name="settle",
+    )(*found)
     return loss.reshape(()), query, cand
 
 

time: 57.4 us -> 55.3 us (0.963)
  local copies, waits for them, and re-layouts: 2.19 us -> 0 us
  between operations: 2.4 us -> 0.64 us
  Pallas kernels: 52.6 us -> 54.1 us
    unnamed x4 -> x0, local copies, waits for them, and re-layouts: 2.19 us -> none
    pallas_call x1 -> x2, Pallas kernels: 52.6 us -> 54.1 us  [the longest x1 51.4 us: on_device(): pl.pallas_call(kernel, out_shape=results, in_specs=[anywhere] * 4, out_sp...]
where the time goes in v4:
time: 55.3 us; the launch traced here: 54.8 us
  Pallas kernels  54.1 us (98%)
  between operations  0.64 us (1%)
    pallas_call x1, Pallas kernels, on_device(): pl.pallas_call(kernel, out_shape=results, in_specs=[anywhere] * 4, out_sp...  51.4 us
    pallas_call x1, Pallas kernels, on_device(): pl.pallas_call(settle, out_shape=results, in_specs=[small, anywhere, anyw...  2.73 us

profile of v4, /device:TPU:1, one launch (start us, length us, event | category | flops | bytes accessed | tf_op | source)
XLA Modules:
  0.0 54.8 jit_solution(284199425585664526)
XLA Ops:
  0.6 51.4 %towers.1 = (f32[1,1]{1,0:T(1,128)}, f32[128,256]{1,0:T(8,128)}, f32[32,256]{1,0:T(8,128)}) custom-call(f32[128,256]{1,0:T(8,128)} %users_hbm.1, f32[32,256]{1,0:T(8,128)} %items_hbm.1, s32[1,32]{1,0:T(1,128)} %bitcast.3, s32[1,128]{1,0:T(1,128)} %bitcast.4), custom_call_target="tpu_custom_call" | custom-call | flops 3221225472 | bytes 524288 | tf_op jit(solution)/shard_map/towers/pallas_call | solution.py:428
  52.0 2.7 %settle.1 = (f32[1,1]{1,0:T(1,128)}, f32[128,256]{1,0:T(8,128)}, f32[32,256]{1,0:T(8,128)}) custom-call(f32[1,1]{1,0:T(1,128)} %get-tuple-element.9.loss_in, f32[128,256]{1,0:T(8,128)} %get-tuple-element.10.query_in, f32[32,256]{1,0:T(8,128)} %get-tuple-element.11.cand_in), custom_call_target="tpu_custom_call" | custom-call | tf_op jit(solution)/shard_map/settle/pallas_call | solution.py:476

commit v5 on v4

--- a/solution.py
+++ b/solution.py
@@ -92,9 +92,19 @@
 
     pl.semaphore_wait(barrier, NZ + NY + NX - 3 + 1)
 
-    def z_copy(d):
-        s = SLOT[(NZ - d) % NZ]
-        return copy(rows.at[0], rows.at[s], Z_S, z_rs.at[s // 2], dz=d)
+    def z_copy(d, origin=0, part=slice(0, UD)):
+        s = SLOT[(NZ + origin - d) % NZ]
+        src = rows.at[SLOT[origin], part]
+        return copy(src, rows.at[s, part], Z_S, z_rs.at[s], dz=d)
+
+    def z_forward():
+        for origin, near, far, part in (
+            (6, 1, 2, slice(0, UD // 2)),
+            (2, 7, 6, slice(UD // 2, UD)),
+        ):
+            whole(rows.at[SLOT[origin]], z_rs.at[SLOT[origin]])
+            z_copy(far, origin, part).start()
+            z_copy(near, origin).start()
 
     def y_copy(d):
         s = SLOT[(NY - d) % NY]
@@ -131,7 +141,7 @@
         x_copy(0, e).start()
     loads[2].wait()
     rows[0] = users_ref[...].astype(BF16)
-    for d in ORDER[1:]:
+    for d in (2, 6, 1, 7):
         z_copy(d).start()
 
     def forward(s):
@@ -146,6 +156,7 @@
         qx_copy(e).start()
     for s in range(4, 8):
         forward(s)
+    z_forward()
 
     first = (b * 16 + g) * ID
     loads[3].wait()
@@ -210,7 +221,8 @@
             acc[blk, ORDER[2 * k + i]] = part[:, i * UD : (i + 1) * UD]
 
     def wait_users(k):
-        whole(rows.at[max(2 * k, 1) : 2 * k + 2], z_rs.at[k])
+        for s in ((1,), (2,), (5,), (6, 7))[k]:
+            whole(rows.at[s], z_rs.at[s])
 
     def wait_other(k):
         row, n = ((0, 512), (512, 256), (768, 256))[k]
@@ -462,7 +474,7 @@
             pltpu.VMEM((11, 8, 128), F32),
             pltpu.VMEM((ID, D), F32),
             pltpu.VMEM((D, UD), F32),
-            dma(15), dma(NZ // 2), dma(NY), dma(NY), dma(3), dma(4), dma(NY), dma(9), dma(2),
+            dma(15), dma(NZ), dma(NY), dma(NY), dma(3), dma(4), dma(NY), dma(9), dma(2),
         ],
         compiler_params=pltpu.CompilerParams(
             collective_id=0, has_side_effects=True, vmem_limit_bytes=64 * 2**20

time: 55.3 us -> 53.1 us (0.960)
  Pallas kernels: 54.1 us -> 52.3 us
    pallas_call x1, Pallas kernels: 51.4 us -> 49.6 us  [on_device(): pl.pallas_call(kernel, out_shape=results, in_specs=[anywhere] * 4, out_sp...]
where the time goes in v5:
time: 53.1 us; the launch traced here: 52.9 us
  Pallas kernels  52.3 us (98%)
  between operations  0.64 us (1%)
    pallas_call x1, Pallas kernels, on_device(): pl.pallas_call(kernel, out_shape=results, in_specs=[anywhere] * 4, out_sp...  49.6 us
    pallas_call x1, Pallas kernels, on_device(): pl.pallas_call(settle, out_shape=results, in_specs=[small, anywhere, anyw...  2.73 us

profile of v5, /device:TPU:1, one launch (start us, length us, event | category | flops | bytes accessed | tf_op | source)
XLA Modules:
  0.0 52.9 jit_solution(9885481041656207566)
XLA Ops:
  0.6 49.6 %towers.1 = (f32[1,1]{1,0:T(1,128)}, f32[128,256]{1,0:T(8,128)}, f32[32,256]{1,0:T(8,128)}) custom-call(f32[128,256]{1,0:T(8,128)} %users_hbm.1, f32[32,256]{1,0:T(8,128)} %items_hbm.1, s32[1,32]{1,0:T(1,128)} %bitcast.3, s32[1,128]{1,0:T(1,128)} %bitcast.4), custom_call_target="tpu_custom_call" | custom-call | flops 3221225472 | bytes 524288 | tf_op jit(solution)/shard_map/towers/pallas_call | solution.py:440
  50.2 2.7 %settle.1 = (f32[1,1]{1,0:T(1,128)}, f32[128,256]{1,0:T(8,128)}, f32[32,256]{1,0:T(8,128)}) custom-call(f32[1,1]{1,0:T(1,128)} %get-tuple-element.9.loss_in, f32[128,256]{1,0:T(8,128)} %get-tuple-element.10.query_in, f32[32,256]{1,0:T(8,128)} %get-tuple-element.11.cand_in), custom_call_target="tpu_custom_call" | custom-call | tf_op jit(solution)/shard_map/settle/pallas_call | solution.py:488

commit v6 on v5

--- a/solution.py
+++ b/solution.py
@@ -30,8 +30,8 @@
 
 def kernel(
     users_hbm, items_hbm, counts_hbm, tgt_hbm,
-    loss_ref, query_hbm, cand_hbm,
-    query_ref, cand_ref,
+    loss_hbm, query_hbm, cand_hbm,
+    loss_ref, query_ref, cand_ref,
     users_ref, items_ref, counts_ref, tgt_ref, in_sem,
     rows, it, lq, it_t, lqc, p_all, acc, mst, lst, st_out, st_in, pt_out, pt_in,
     w_row, own_f, ip, xc_in, xs_in, ys_out, ys_in, loss_out, loss_in, tq_s, tv_s,
@@ -343,6 +343,11 @@
 
     for c in (3, 2, 1, 0):
         xc_copy(c).wait_recv()
+        if c == 3:
+            whole(loss_in.at[0], L0_R)
+            loss_out[1] = loss_out[0] + loss_in[0]
+            for e in range(1, NX):
+                ls_copy(1, e, dx=e).start()
         for k in (2 * c + 1, 2 * c):
             spot = slice(k * NX * ID, (k + 1) * NX * ID)
             total = own_f[spot, :] + xc_in[spot, :].astype(F32)
@@ -351,10 +356,6 @@
             for e in (2, 1, 3):
                 xs_copy(k, e).start()
 
-    whole(loss_in.at[0], L0_R)
-    loss_out[1] = loss_out[0] + loss_in[0]
-    for e in range(1, NX):
-        ls_copy(1, e, dx=e).start()
 
     def ys_copy(s):
         mirror = SLOT[(NY - ORDER[s]) % NY]
@@ -370,10 +371,11 @@
     for s in range(NY - 1, 0, -1):
         ys_out[s] = x_total(s).astype(BF16)
         ys_copy(s).start()
-    whole(loss_in.at[1:NX], L1_R)
-    loss_out[2] = loss_out[1] + loss_in[1] + loss_in[2] + loss_in[3]
-    for d in range(1, NY):
-        ls_copy(2, 3 + d, dy=d).start()
+        if s == 6:
+            whole(loss_in.at[1:NX], L1_R)
+            loss_out[2] = loss_out[1] + loss_in[1] + loss_in[2] + loss_in[3]
+            for d in (4, 3, 5, 2, 6, 1, 7):
+                ls_copy(2, 3 + d, dy=d).start()
     cand = x_total(0) - tq_s[...]
 
     user_sum = part_of(0) * share[0] - tv_s[...]
@@ -401,27 +403,27 @@
     for d in range(1, NY):
         total = total + loss_in[3 + d]
     loss_ref[...] = total[0:1, 0:1] * (1.0 / (2 * NX * NY * NZ * UD))
+    loss_left = pltpu.make_async_copy(loss_ref, loss_hbm, out_sem.at[2])
+    loss_left.start()
 
     whole(ys_in.at[1:NY], YS_S)
     whole(loss_in.at[4:11], L2_S)
     query_out.wait()
     cand_out.wait()
+    loss_left.wait()
 
 
 def settle(
-    loss_in, query_in, cand_in, loss_out, query_out, cand_out, query_v, cand_v, in_sem, out_sem
+    loss_in, query_in, cand_in, loss_out, query_out, cand_out,
+    loss_v, query_v, cand_v, in_sem, out_sem,
 ):
-    ins = [
-        pltpu.make_async_copy(query_in, query_v, in_sem.at[0]),
-        pltpu.make_async_copy(cand_in, cand_v, in_sem.at[1]),
-    ]
-    outs = [
-        pltpu.make_async_copy(query_v, query_out, out_sem.at[0]),
-        pltpu.make_async_copy(cand_v, cand_out, out_sem.at[1]),
-    ]
+    way = (
+        (query_in, query_v, query_out), (cand_in, cand_v, cand_out), (loss_in, loss_v, loss_out)
+    )
+    ins = [pltpu.make_async_copy(a, v, in_sem.at[k]) for k, (a, v, _) in enumerate(way)]
+    outs = [pltpu.make_async_copy(v, b, out_sem.at[k]) for k, (_, v, b) in enumerate(way)]
     for move in ins:
         move.start()
-    loss_out[...] = loss_in[...]
     for arrival, departure in zip(ins, outs):
         arrival.wait()
         departure.start()
@@ -441,8 +443,9 @@
         kernel,
         out_shape=results,
         in_specs=[anywhere] * 4,
-        out_specs=(pl.BlockSpec(memory_space=pltpu.VMEM), anywhere, anywhere),
+        out_specs=(anywhere,) * 3,
         scratch_shapes=[
+            pltpu.VMEM((1, 1), F32),
             pltpu.VMEM((UD, D), F32),
             pltpu.VMEM((ID, D), F32),
             pltpu.VMEM((UD, D), F32),
@@ -474,7 +477,7 @@
             pltpu.VMEM((11, 8, 128), F32),
             pltpu.VMEM((ID, D), F32),
             pltpu.VMEM((D, UD), F32),
-            dma(15), dma(NZ), dma(NY), dma(NY), dma(3), dma(4), dma(NY), dma(9), dma(2),
+            dma(15), dma(NZ), dma(NY), dma(NY), dma(3), dma(4), dma(NY), dma(9), dma(3),
         ],
         compiler_params=pltpu.CompilerParams(
             collective_id=0, has_side_effects=True, vmem_limit_bytes=64 * 2**20
@@ -484,13 +487,14 @@
         ),
         name="towers",
     )(users, items, counts.reshape(1, ID), target_indices.reshape(1, UD))
-    small = pl.BlockSpec(memory_space=pltpu.VMEM)
     loss, query, cand = pl.pallas_call(
         settle,
         out_shape=results,
-        in_specs=[small, anywhere, anywhere],
-        out_specs=(small, anywhere, anywhere),
-        scratch_shapes=[pltpu.VMEM((UD, D), F32), pltpu.VMEM((ID, D), F32), dma(2), dma(2)],
+        in_specs=[anywhere] * 3,
+        out_specs=(anywhere,) * 3,
+        scratch_shapes=[
+            pltpu.VMEM((1, 1), F32), pltpu.VMEM((UD, D), F32), pltpu.VMEM((ID, D), F32), dma(3), dma(3)
+        ],
         compiler_params=pltpu.CompilerParams(vmem_limit_bytes=64 * 2**20),
         name="settle",
     )(*found)

time: 53.1 us -> 52.2 us (0.983)
  Pallas kernels: 52.3 us -> 51.4 us
where the time goes in v6:
time: 52.2 us; the launch traced here: 52.1 us
  Pallas kernels  51.4 us (98%)
  between operations  0.64 us (1%)
    pallas_call x1, Pallas kernels, on_device(): pl.pallas_call(kernel, out_shape=results, in_specs=[anywhere] * 4, out_sp...  49.2 us
    pallas_call x1, Pallas kernels, on_device(): pl.pallas_call(settle, out_shape=results, in_specs=[anywhere] * 3, out_sp...  2.23 us

profile of v6, /device:TPU:1, one launch (start us, length us, event | category | flops | bytes accessed | tf_op | source)
XLA Modules:
  0.0 52.1 jit_solution(882046386771957394)
XLA Ops:
  0.6 49.2 %towers.1 = (f32[1,1]{1,0:T(1,128)}, f32[128,256]{1,0:T(8,128)}, f32[32,256]{1,0:T(8,128)}) custom-call(f32[128,256]{1,0:T(8,128)} %users_hbm.1, f32[32,256]{1,0:T(8,128)} %items_hbm.1, s32[1,32]{1,0:T(1,128)} %bitcast.3, s32[1,128]{1,0:T(1,128)} %bitcast.4), custom_call_target="tpu_custom_call" | custom-call | flops 3221225472 | bytes 524288 | tf_op jit(solution)/shard_map/towers/pallas_call | solution.py:442
  49.8 2.2 %settle.1 = (f32[1,1]{1,0:T(1,128)}, f32[128,256]{1,0:T(8,128)}, f32[32,256]{1,0:T(8,128)}) custom-call(f32[1,1]{1,0:T(1,128)} %get-tuple-element.9.loss_in, f32[128,256]{1,0:T(8,128)} %get-tuple-element.10.query_in, f32[32,256]{1,0:T(8,128)} %get-tuple-element.11.cand_in), custom_call_target="tpu_custom_call" | custom-call | tf_op jit(solution)/shard_map/settle/pallas_call | solution.py:490

commit v7 on v6

--- a/solution.py
+++ b/solution.py
@@ -75,9 +75,9 @@
         load.start()
 
     barrier = pltpu.get_barrier_semaphore()
-    for d in range(1, NZ):
+    for d in (4, 3, 5, 2, 6, 1, 7):
         pl.semaphore_signal(barrier, inc=1, device_id=device(dz=d), device_id_type=MESH)
-    for d in range(1, NY):
+    for d in (4, 3, 5, 2, 6, 1, 7):
         pl.semaphore_signal(barrier, inc=1, device_id=device(dy=d), device_id_type=MESH)
     for d in range(1, NX):
         pl.semaphore_signal(barrier, inc=1, device_id=device(dx=d), device_id_type=MESH)
@@ -146,7 +146,7 @@
 
     def forward(s):
         whole(it.at[0, pl.ds(s * NX * ID, ID)], y_rs.at[s])
-        for e in range(1, NX):
+        for e in (2, 1, 3):
             x_copy(s, e).start()
 
     for s in range(1, 4):

time: 52.2 us -> 52.3 us (level)
  no operation moved by 1% of the time
where the time goes in v7:
time: 52.3 us; the launch traced here: 52.2 us
  Pallas kernels  51.5 us (98%)
  between operations  0.64 us (1%)
    pallas_call x1, Pallas kernels, on_device(): pl.pallas_call(kernel, out_shape=results, in_specs=[anywhere] * 4, out_sp...  49.3 us
    pallas_call x1, Pallas kernels, on_device(): pl.pallas_call(settle, out_shape=results, in_specs=[anywhere] * 3, out_sp...  2.23 us

profile of v7, /device:TPU:1, one launch (start us, length us, event | category | flops | bytes accessed | tf_op | source)
XLA Modules:
  0.0 52.2 jit_solution(4246241082942990525)
XLA Ops:
  0.6 49.3 %towers.1 = (f32[1,1]{1,0:T(1,128)}, f32[128,256]{1,0:T(8,128)}, f32[32,256]{1,0:T(8,128)}) custom-call(f32[128,256]{1,0:T(8,128)} %users_hbm.1, f32[32,256]{1,0:T(8,128)} %items_hbm.1, s32[1,32]{1,0:T(1,128)} %bitcast.3, s32[1,128]{1,0:T(1,128)} %bitcast.4), custom_call_target="tpu_custom_call" | custom-call | flops 3221225472 | bytes 524288 | tf_op jit(solution)/shard_map/towers/pallas_call | solution.py:442
  49.9 2.2 %settle.1 = (f32[1,1]{1,0:T(1,128)}, f32[128,256]{1,0:T(8,128)}, f32[32,256]{1,0:T(8,128)}) custom-call(f32[1,1]{1,0:T(1,128)} %get-tuple-element.9.loss_in, f32[128,256]{1,0:T(8,128)} %get-tuple-element.10.query_in, f32[32,256]{1,0:T(8,128)} %get-tuple-element.11.cand_in), custom_call_target="tpu_custom_call" | custom-call | tf_op jit(solution)/shard_map/settle/pallas_call | solution.py:490
